TPU v7x, 512 devices: a whole 4x8x8 slice. The times are simulated.
512 devices in a mesh: ctx: 64 (over y, x, z_hi), ch: 8 (over z_lo, core).
Axes of the slice: x: 4, y: 8, z: 8 (z_hi: 2, z_lo: 4; z = z_hi * 4 + z_lo), core: 2. Of those that a mesh axis runs over, the one named last changes fastest.
Arguments:
- queries: bfloat16 [8192, 1024], P('ctx', 'ch'), may hold values from -5 to 5
- keys_in: bfloat16 [8192, 1024], P('ctx', 'ch'), may hold values from -5 to 5
- values: bfloat16 [8192, 1024], P('ctx', 'ch'), may hold values from -12 to 12
- hyena_query: bfloat16 [8192, 1024], P('ctx', 'ch'), may hold values from -3 to 3
- hyena_value: bfloat16 [8192, 1024], P('ctx', 'ch'), may hold values from -3 to 3
- filter_taps: bfloat16 [8192, 1024], P('ctx', 'ch'), may hold values from -6 to 6
- norm_gain: float32 [1024], P('ch'), may hold values from 0.5 to 1.5
- upstream: bfloat16 [8192, 1024], P('ctx', 'ch'), may hold values from -3 to 3
- block_order: int32 [128], replicated, may hold values from 0 to 127, each once
Outputs:
- grad_queries: bfloat16 [8192, 1024], P('ctx', 'ch')
- grad_keys: bfloat16 [8192, 1024], P('ctx', 'ch')
- grad_values: bfloat16 [8192, 1024], P('ctx', 'ch')
- grad_hyena_query: bfloat16 [8192, 1024], P('ctx', 'ch')
- grad_hyena_value: bfloat16 [8192, 1024], P('ctx', 'ch')
- grad_taps: bfloat16 [8192, 1024], P('ctx', 'ch')
Inputs may be any that keep to these rules, and one draw needn't show every extreme that they name: block_order[j] is the sequence block of 64 positions that stored rows j * 64 to (j + 1) * 64 - 1 hold; each block once.
All inputs are finite; a program needn't handle non-finite values.
Results may differ from a plain program's by a relative error of at most 0.039.
Values may be sent and summed in bfloat16 or wider, within the bound.
A program may use at most 64 MiB of HBM per device.

v0:
```python
from functools import partial
import math

import jax
import jax.numpy as jnp
from jax import lax
from jax.sharding import PartitionSpec as P

HEAD_DIM = 128


HIGHEST = lax.Precision.HIGHEST


def passed_along(value, axis, steps):
    count = lax.axis_size(axis)
    pairs = [(source, (source + steps) % count) for source in range(count)]
    return lax.ppermute(value, axis, pairs)


def stored_positions(block_order, first_row, count, half):
    rows = first_row + jnp.arange(count, dtype=jnp.int32)
    return jnp.take(block_order, rows // half) * half + rows % half


def tile_scores(queries, keys, query_pos, key_pos, scale):
    scores = jnp.einsum("qhd,khd->hqk", queries, keys, preferred_element_type=jnp.float32) * scale
    visible = key_pos[None, :] <= query_pos[:, None]
    return (scores, visible[None])


def forward_fold(carry, pieces, start, queries, query_pos, block_order, half, scale):
    keys, values = pieces
    count = keys.shape[0]
    heads = queries.shape[1]
    keys = keys.reshape(count, heads, -1)
    values = values.reshape(count, heads, -1)
    key_pos = stored_positions(block_order, start, count, half)
    scores, visible = tile_scores(queries, keys, query_pos, key_pos, scale)
    scores = jnp.where(visible, scores, -jnp.inf)
    peak, total, accum = carry
    new_peak = jnp.max(scores, axis=2)
    anchor = jnp.where(jnp.isfinite(new_peak), new_peak, 0.0)
    weights = jnp.exp(scores - anchor[:, :, None])
    factor = jnp.exp(peak - anchor)
    total = total * factor + jnp.sum(weights, axis=2)
    accum = accum * factor[:, :, None] + jnp.einsum(
        "hqk,khd->hqd", weights.astype(jnp.bfloat16), values, preferred_element_type=jnp.float32
    )
    return (new_peak, total, accum)


def tile_grads(queries, douts, lse, delta, query_pos, keys, values, key_pos, scale):
    scores, visible = tile_scores(queries, keys, query_pos, key_pos, scale)
    probs = jnp.exp(jnp.where(visible, scores - lse[:, :, None], -jnp.inf))
    dprobs = jnp.einsum("qhd,khd->hqk", douts, values, preferred_element_type=jnp.float32)
    dscores = (probs * (dprobs - delta[:, :, None])).astype(jnp.bfloat16)
    probs_low = probs.astype(jnp.bfloat16)
    grad_query = (
        jnp.einsum("hqk,khd->qhd", dscores, keys, preferred_element_type=jnp.float32) * scale
    )
    grad_key = (
        jnp.einsum("hqk,qhd->khd", dscores, queries, preferred_element_type=jnp.float32) * scale
    )
    grad_value = jnp.einsum("hqk,qhd->khd", probs_low, douts, preferred_element_type=jnp.float32)
    return (grad_query, grad_key, grad_value)


def phase_table(count_first, count_second, modulus):
    first = jnp.arange(count_first, dtype=jnp.int32)[:, None]
    second = jnp.arange(count_second, dtype=jnp.int32)[None, :]
    angle = 2.0 * math.pi / modulus * (first * second % modulus).astype(jnp.float32)
    return (jnp.cos(angle), jnp.sin(angle))


def spectral_tables(length):
    column_count = 128
    row_count = length // column_count
    row_cos, row_sin = phase_table(row_count, row_count, row_count)
    twist_cos, twist_sin = phase_table(row_count, column_count, length)
    col_cos, col_sin = phase_table(column_count, column_count, column_count)
    return (row_cos, row_sin, twist_cos, twist_sin, col_cos, col_sin)


def complex_left(mat_real, mat_imag, real, imag):
    product = partial(jnp.einsum, "ij,cjq->ciq", precision=HIGHEST)
    return (
        product(mat_real, real) - product(mat_imag, imag),
        product(mat_real, imag) + product(mat_imag, real),
    )


def complex_right(real, imag, mat_real, mat_imag):
    product = partial(jnp.einsum, "cij,jq->ciq", precision=HIGHEST)
    return (
        product(real, mat_real) - product(imag, mat_imag),
        product(real, mat_imag) + product(imag, mat_real),
    )


def forward_dft(real, imag, tables):
    row_cos, row_sin, twist_cos, twist_sin, col_cos, col_sin = tables
    real, imag = complex_left(row_cos, -row_sin, real, imag)
    real, imag = (real * twist_cos + imag * twist_sin, imag * twist_cos - real * twist_sin)
    return complex_right(real, imag, col_cos, -col_sin)


def inverse_dft(real, imag, tables, length):
    row_cos, row_sin, twist_cos, twist_sin, col_cos, col_sin = tables
    real, imag = complex_right(real, imag, col_cos, col_sin)
    real, imag = (real * twist_cos - imag * twist_sin, imag * twist_cos + real * twist_sin)
    real, imag = complex_left(row_cos, row_sin, real, imag)
    return real / length


def per_device(
    queries,
    keys_in,
    values,
    hyena_query,
    hyena_value,
    filter_taps,
    norm_gain,
    upstream,
    block_order,
):
    tok_rows, local_width = queries.shape
    cycle_size = lax.axis_size("ctx")
    width = local_width * lax.axis_size("ch")
    heads = local_width // HEAD_DIM
    half = tok_rows // 2
    seq_len = tok_rows * cycle_size
    scale = 1.0 / math.sqrt(HEAD_DIM)
    device = lax.axis_index("ctx")
    query_pos = stored_positions(block_order, device * tok_rows, tok_rows, half)
    query_heads = queries.reshape(tok_rows, heads, HEAD_DIM)
    key_heads = keys_in.reshape(tok_rows, heads, HEAD_DIM)
    value_heads = values.reshape(tok_rows, heads, HEAD_DIM)
    start_state = (
        jnp.full((heads, tok_rows), -jnp.inf, jnp.float32),
        jnp.zeros((heads, tok_rows), jnp.float32),
        jnp.zeros((heads, tok_rows, HEAD_DIM), jnp.float32),
    )
    folder = partial(
        forward_fold,
        queries=query_heads,
        query_pos=query_pos,
        block_order=block_order,
        half=half,
        scale=scale,
    )
    fold_state = folder(
        start_state,
        (
            lax.all_gather(keys_in, "ctx", axis=0, tiled=True),
            lax.all_gather(values, "ctx", axis=0, tiled=True),
        ),
        jnp.int32(0),
    )
    peak, total, accum = (fold_state[0], fold_state[1], fold_state[2])
    lse = peak + jnp.log(total)
    attended = (
        (accum / total[:, :, None])
        .transpose(1, 0, 2)
        .reshape(tok_rows, local_width)
        .astype(jnp.bfloat16)
    )
    act = attended.astype(jnp.float32)
    square_sum = lax.psum(jnp.sum(act * act, axis=1), "ch")
    inv_root = lax.rsqrt(square_sum[:, None] / width + 1e-06)
    normed = act * inv_root * norm_gain
    mixed = (normed * hyena_value.astype(jnp.float32)).astype(jnp.bfloat16)
    gated = (upstream.astype(jnp.float32) * hyena_query.astype(jnp.float32)).astype(jnp.bfloat16)
    mixed_cols, gated_cols, taps_cols = (
        lax.all_to_all(mixed, "ctx", split_axis=1, concat_axis=0, tiled=True),
        lax.all_to_all(gated, "ctx", split_axis=1, concat_axis=0, tiled=True),
        lax.all_to_all(filter_taps, "ctx", split_axis=1, concat_axis=0, tiled=True),
    )
    count = 2 * cycle_size
    inverse = jnp.zeros((count,), jnp.int32).at[block_order].set(jnp.arange(count, dtype=jnp.int32))

    def reorder(field, index):
        return field.reshape(count, half, -1)[index].reshape(seq_len, -1)

    length = 2 * seq_len
    row_count = length // 128
    tables = spectral_tables(length)

    def padded(field):
        wide = jnp.concatenate([field, jnp.zeros_like(field)], axis=1)
        return wide.reshape(field.shape[0], row_count, 128)

    def spectrum(field):
        grid = padded(field)
        return forward_dft(grid, jnp.zeros_like(grid), tables)

    def back_to_lines(real, imag):
        line = inverse_dft(real, imag, tables, length)
        return line.reshape(line.shape[0], length)[:, :seq_len].T

    mixed_true = reorder(mixed_cols, inverse).T.astype(jnp.float32)
    gated_true = reorder(gated_cols, inverse).T.astype(jnp.float32)
    taps = taps_cols.T.astype(jnp.float32) * seq_len ** (-0.5)
    mix_real, mix_imag = spectrum(mixed_true)
    tap_real, tap_imag = spectrum(taps)
    grad_real, grad_imag = spectrum(gated_true)
    conv = back_to_lines(
        tap_real * mix_real - tap_imag * mix_imag, tap_real * mix_imag + tap_imag * mix_real
    )
    back_mixed = back_to_lines(
        tap_real * grad_real + tap_imag * grad_imag, tap_real * grad_imag - tap_imag * grad_real
    )
    back_taps = back_to_lines(
        mix_real * grad_real + mix_imag * grad_imag, mix_real * grad_imag - mix_imag * grad_real
    )
    conv_cols = reorder(conv, block_order).astype(jnp.bfloat16)
    back_cols = reorder(back_mixed, block_order).astype(jnp.bfloat16)
    taps_grad = (back_taps * seq_len ** (-0.5)).astype(jnp.bfloat16)
    conv_rows, back_rows, grad_taps = (
        lax.all_to_all(conv_cols, "ctx", split_axis=0, concat_axis=1, tiled=True),
        lax.all_to_all(back_cols, "ctx", split_axis=0, concat_axis=1, tiled=True),
        lax.all_to_all(taps_grad, "ctx", split_axis=0, concat_axis=1, tiled=True),
    )
    grad_hyena_query = (upstream.astype(jnp.float32) * conv_rows.astype(jnp.float32)).astype(
        jnp.bfloat16
    )
    back_wide = back_rows.astype(jnp.float32)
    grad_hyena_value = (back_wide * normed).astype(jnp.bfloat16)
    scaled = back_wide * hyena_value.astype(jnp.float32) * norm_gain
    inner = lax.psum(jnp.sum(scaled * act, axis=1), "ch")
    grad_attended = (inv_root * scaled - act * inv_root**3 * (inner[:, None] / width)).astype(
        jnp.bfloat16
    )
    douts = grad_attended.reshape(tok_rows, heads, HEAD_DIM)
    delta = jnp.sum(
        (grad_attended.astype(jnp.float32) * act).reshape(tok_rows, heads, HEAD_DIM), axis=2
    ).T
    empty = jnp.zeros((tok_rows, heads, HEAD_DIM), jnp.float32)

    def advance(turn, state):
        moving_keys, moving_values, grad_keys, grad_values, grad_query = state
        source = (device - turn) % cycle_size
        key_pos = stored_positions(block_order, source * tok_rows, tok_rows, half)
        part_query, part_key, part_value = tile_grads(
            query_heads, douts, lse, delta, query_pos, moving_keys, moving_values, key_pos, scale
        )
        moving_keys, moving_values = passed_along((moving_keys, moving_values), "ctx", 1)
        grad_keys, grad_values = passed_along(
            (grad_keys + part_key, grad_values + part_value), "ctx", 1
        )
        return (moving_keys, moving_values, grad_keys, grad_values, grad_query + part_query)

    final = lax.fori_loop(0, cycle_size, advance, (key_heads, value_heads, empty, empty, empty))
    grad_keys, grad_values, grad_query = (final[2], final[3], final[4])
    return (
        grad_query.reshape(tok_rows, local_width).astype(jnp.bfloat16),
        grad_keys.reshape(tok_rows, local_width).astype(jnp.bfloat16),
        grad_values.reshape(tok_rows, local_width).astype(jnp.bfloat16),
        grad_hyena_query,
        grad_hyena_value,
        grad_taps,
    )


def solution(mesh):
    return jax.shard_map(
        per_device,
        mesh=mesh,
        in_specs=(
            P("ctx", "ch"),
            P("ctx", "ch"),
            P("ctx", "ch"),
            P("ctx", "ch"),
            P("ctx", "ch"),
            P("ctx", "ch"),
            P("ch"),
            P("ctx", "ch"),
            P(),
        ),
        out_specs=(
            P("ctx", "ch"),
            P("ctx", "ch"),
            P("ctx", "ch"),
            P("ctx", "ch"),
            P("ctx", "ch"),
            P("ctx", "ch"),
        ),
        check_vma=False,
    )
```

profile of v0, /device:TPU:70, one launch (start us, length us, event | category | flops | bytes accessed | tf_op | source)
XLA Modules:
  0.0 2241.7 jit_solution(7174774636506344939)
XLA Ops:
  12.4 18.1 all-to-all-start.1
  37.9 48.9 %gather_fusion.1 = s32[8192]{0:T(1024)S(1)} fusion(s32[128]{0:T(128)S(1)} %copy-done, s32[8192]{0:T(1024)S(1)} %broadcast_clamp_fusion), kind=kCustom, calls=%fused_computation.2 | custom fusion | bytes 98304 | tf_op jit(solution)/shard_map/jit(_take)/gather | solution.py:23
  86.8 15.1 all-to-all-start
  105.2 9.3 all-to-all-done
  131.0 12.5 all-to-all-done.2
  143.6 11.8 all-gather.3.cloned.1.call-done
  159.8 133.0 %all-gather.5.cloned.1.call-done = bf16[8192,128]{1,0:T(8,128)(2,1)} async-done(((bf16[128,128]{1,0:T(8,128)(2,1)}), bf16[8192,128]{1,0:T(8,128)(2,1)}) %all-gather.5.cloned.1.call-update) | async-done | bytes 2097168 | tf_op jit(solution)/shard_map/all_gather | solution.py:156
  296.8 10.8 all-reduce.3
  316.2 1861.6 %while.24 = (s32[]{:T(128)}, bf16[128,1,128]{2,0,1:T(8,128)(2,1)S(1)}, bf16[128,1,128]{2,0,1:T(8,128)(2,1)S(1)}, f32[128,1,128]{2,0,1:T(8,128)S(1)}, f32[128,1,1...) while((s32[]{:T(128)}, ...), condition=%wide.region_9.11_spmd.clone, body=%wide.region_8.10_spmd.clone.sunk | while | flops 21208080 | bytes 1845212 | solution.py:253
  350.4 9.7 collective-permute-start.1
  406.6 10.3 collective-permute-start.1
  682.8 9.0 collective-permute-start.3
  843.6 10.3 collective-permute-start.1
  900.3 9.4 collective-permute-start.1
  1367.8 10.1 collective-permute-start.1
  1436.4 9.2 collective-permute-start.3
  1484.5 9.4 collective-permute-start.1
  1712.6 9.5 collective-permute-start.1
  1728.2 9.6 collective-permute-start.3
  1921.7 9.9 collective-permute-start.1
  2021.8 9.5 collective-permute-start.3
  2134.8 9.1 collective-permute-start.3
  2188.7 13.3 all-to-all-start.5
  2223.6 10.5 all-to-all-done.4
  (1349 shorter events, 1809.1 us)
Async XLA Ops:
  7.2 148.2 %all-gather.3.cloned.1.call-start = ((), (), s32[]{:S(2)}) async-start(), calls=%async_computation.6 | async-start | bytes 2129920 | tf_op jit(solution)/shard_map/all_gather | solution.py:155
  12.4 74.4 %all-to-all-start.1 = ((bf16[128,64,2]{0,2,1:T(2,128)(2,1)}), bf16[128,64,2]{0,2,1:T(2,128)(2,1)S(1)}, u32[]{:S(2)}, u32[]{:S(2)}) async-start(bf16[128,64,2]{0,2,1:T(2,128)(2,1)} %bitcast.14), calls=%async_computation.1 | async-start | bytes 65536 | tf_op jit(solution)/shard_map/all_to_all | solution.py:176
  30.5 262.2 %all-gather.5.cloned.1.call-start = ((), (), s32[]{:S(2)}) async-start(), calls=%async_computation.7 | async-start | bytes 2129920 | tf_op jit(solution)/shard_map/all_gather | solution.py:156
  86.8 27.7 %all-to-all-start = ((bf16[128,64,2]{0,2,1:T(2,128)(2,1)}), bf16[128,64,2]{0,2,1:T(2,128)(2,1)S(1)}, u32[]{:S(2)}, u32[]{:S(2)}) async-start(bf16[128,64,2]{0,2,1:T(2,128)(2,1)} %bitcast.6), calls=%async_computation | async-start | bytes 65536 | tf_op jit(solution)/shard_map/all_to_all | solution.py:177
  308.4 1870.6 %all-to-all-start.3 = ((bf16[128,64,2]{0,2,1:T(2,128)(2,1)}), bf16[128,64,2]{0,2,1:T(2,128)(2,1)S(1)}, u32[]{:S(2)}, u32[]{:S(2)}) async-start(bf16[128,64,2]{0,2,1:T(2,128)(2,1)} %bitcast.29), calls=%async_computation.3 | async-start | bytes 65536 | tf_op jit(solution)/shard_map/all_to_all | solution.py:175
  489.1 25.7 %collective-permute-start = (bf16[128,1,128]{2,0,1:T(8,128)(2,1)S(1)}, bf16[128,1,128]{2,0,1:T(8,128)(2,1)S(1)}, u32[]{:S(2)}, u32[]{:S(2)}) collective-permute-start(bf16[128,1,128]{2,0,1:T(8,128)(2,1)S(1)} %copy.339), channel_id=1, source_target_pairs={{0,8},{8,16},{16,24},{24,32},{32,40},{40,48},{48,56},{56,64},{64,7... | collective-permute-start | bytes 98312 | tf_op jit(solution)/shard_map/while/body/eval_jaxpr/ppermute | solution.py:18
  547.0 26.8 %collective-permute-start = (bf16[128,1,128]{2,0,1:T(8,128)(2,1)S(1)}, bf16[128,1,128]{2,0,1:T(8,128)(2,1)S(1)}, u32[]{:S(2)}, u32[]{:S(2)}) collective-permute-start(bf16[128,1,128]{2,0,1:T(8,128)(2,1)S(1)} %copy.339), channel_id=1, source_target_pairs={{0,8},{8,16},{16,24},{24,32},{32,40},{40,48},{48,56},{56,64},{64,7... | collective-permute-start | bytes 98312 | tf_op jit(solution)/shard_map/while/body/eval_jaxpr/ppermute | solution.py:18
  578.8 26.4 %collective-permute-start = (bf16[128,1,128]{2,0,1:T(8,128)(2,1)S(1)}, bf16[128,1,128]{2,0,1:T(8,128)(2,1)S(1)}, u32[]{:S(2)}, u32[]{:S(2)}) collective-permute-start(bf16[128,1,128]{2,0,1:T(8,128)(2,1)S(1)} %copy.339), channel_id=1, source_target_pairs={{0,8},{8,16},{16,24},{24,32},{32,40},{40,48},{48,56},{56,64},{64,7... | collective-permute-start | bytes 98312 | tf_op jit(solution)/shard_map/while/body/eval_jaxpr/ppermute | solution.py:18
  724.0 25.7 %collective-permute-start = (bf16[128,1,128]{2,0,1:T(8,128)(2,1)S(1)}, bf16[128,1,128]{2,0,1:T(8,128)(2,1)S(1)}, u32[]{:S(2)}, u32[]{:S(2)}) collective-permute-start(bf16[128,1,128]{2,0,1:T(8,128)(2,1)S(1)} %copy.339), channel_id=1, source_target_pairs={{0,8},{8,16},{16,24},{24,32},{32,40},{40,48},{48,56},{56,64},{64,7... | collective-permute-start | bytes 98312 | tf_op jit(solution)/shard_map/while/body/eval_jaxpr/ppermute | solution.py:18
  894.4 28.7 %collective-permute-start = (bf16[128,1,128]{2,0,1:T(8,128)(2,1)S(1)}, bf16[128,1,128]{2,0,1:T(8,128)(2,1)S(1)}, u32[]{:S(2)}, u32[]{:S(2)}) collective-permute-start(bf16[128,1,128]{2,0,1:T(8,128)(2,1)S(1)} %copy.339), channel_id=1, source_target_pairs={{0,8},{8,16},{16,24},{24,32},{32,40},{40,48},{48,56},{56,64},{64,7... | collective-permute-start | bytes 98312 | tf_op jit(solution)/shard_map/while/body/eval_jaxpr/ppermute | solution.py:18
  1037.7 26.1 %collective-permute-start = (bf16[128,1,128]{2,0,1:T(8,128)(2,1)S(1)}, bf16[128,1,128]{2,0,1:T(8,128)(2,1)S(1)}, u32[]{:S(2)}, u32[]{:S(2)}) collective-permute-start(bf16[128,1,128]{2,0,1:T(8,128)(2,1)S(1)} %copy.339), channel_id=1, source_target_pairs={{0,8},{8,16},{16,24},{24,32},{32,40},{40,48},{48,56},{56,64},{64,7... | collective-permute-start | bytes 98312 | tf_op jit(solution)/shard_map/while/body/eval_jaxpr/ppermute | solution.py:18
  1186.7 29.3 %collective-permute-start = (bf16[128,1,128]{2,0,1:T(8,128)(2,1)S(1)}, bf16[128,1,128]{2,0,1:T(8,128)(2,1)S(1)}, u32[]{:S(2)}, u32[]{:S(2)}) collective-permute-start(bf16[128,1,128]{2,0,1:T(8,128)(2,1)S(1)} %copy.339), channel_id=1, source_target_pairs={{0,8},{8,16},{16,24},{24,32},{32,40},{40,48},{48,56},{56,64},{64,7... | collective-permute-start | bytes 98312 | tf_op jit(solution)/shard_map/while/body/eval_jaxpr/ppermute | solution.py:18
  1362.4 26.1 %collective-permute-start = (bf16[128,1,128]{2,0,1:T(8,128)(2,1)S(1)}, bf16[128,1,128]{2,0,1:T(8,128)(2,1)S(1)}, u32[]{:S(2)}, u32[]{:S(2)}) collective-permute-start(bf16[128,1,128]{2,0,1:T(8,128)(2,1)S(1)} %copy.339), channel_id=1, source_target_pairs={{0,8},{8,16},{16,24},{24,32},{32,40},{40,48},{48,56},{56,64},{64,7... | collective-permute-start | bytes 98312 | tf_op jit(solution)/shard_map/while/body/eval_jaxpr/ppermute | solution.py:18
  1447.5 26.5 %collective-permute-start = (bf16[128,1,128]{2,0,1:T(8,128)(2,1)S(1)}, bf16[128,1,128]{2,0,1:T(8,128)(2,1)S(1)}, u32[]{:S(2)}, u32[]{:S(2)}) collective-permute-start(bf16[128,1,128]{2,0,1:T(8,128)(2,1)S(1)} %copy.339), channel_id=1, source_target_pairs={{0,8},{8,16},{16,24},{24,32},{32,40},{40,48},{48,56},{56,64},{64,7... | collective-permute-start | bytes 98312 | tf_op jit(solution)/shard_map/while/body/eval_jaxpr/ppermute | solution.py:18
  1509.6 25.9 %collective-permute-start = (bf16[128,1,128]{2,0,1:T(8,128)(2,1)S(1)}, bf16[128,1,128]{2,0,1:T(8,128)(2,1)S(1)}, u32[]{:S(2)}, u32[]{:S(2)}) collective-permute-start(bf16[128,1,128]{2,0,1:T(8,128)(2,1)S(1)} %copy.339), channel_id=1, source_target_pairs={{0,8},{8,16},{16,24},{24,32},{32,40},{40,48},{48,56},{56,64},{64,7... | collective-permute-start | bytes 98312 | tf_op jit(solution)/shard_map/while/body/eval_jaxpr/ppermute | solution.py:18
  1675.8 26.9 %collective-permute-start = (bf16[128,1,128]{2,0,1:T(8,128)(2,1)S(1)}, bf16[128,1,128]{2,0,1:T(8,128)(2,1)S(1)}, u32[]{:S(2)}, u32[]{:S(2)}) collective-permute-start(bf16[128,1,128]{2,0,1:T(8,128)(2,1)S(1)} %copy.339), channel_id=1, source_target_pairs={{0,8},{8,16},{16,24},{24,32},{32,40},{40,48},{48,56},{56,64},{64,7... | collective-permute-start | bytes 98312 | tf_op jit(solution)/shard_map/while/body/eval_jaxpr/ppermute | solution.py:18
  1704.8 33.2 %collective-permute-start = (bf16[128,1,128]{2,0,1:T(8,128)(2,1)S(1)}, bf16[128,1,128]{2,0,1:T(8,128)(2,1)S(1)}, u32[]{:S(2)}, u32[]{:S(2)}) collective-permute-start(bf16[128,1,128]{2,0,1:T(8,128)(2,1)S(1)} %copy.339), channel_id=1, source_target_pairs={{0,8},{8,16},{16,24},{24,32},{32,40},{40,48},{48,56},{56,64},{64,7... | collective-permute-start | bytes 98312 | tf_op jit(solution)/shard_map/while/body/eval_jaxpr/ppermute | solution.py:18
  1795.8 28.3 %collective-permute-start = (bf16[128,1,128]{2,0,1:T(8,128)(2,1)S(1)}, bf16[128,1,128]{2,0,1:T(8,128)(2,1)S(1)}, u32[]{:S(2)}, u32[]{:S(2)}) collective-permute-start(bf16[128,1,128]{2,0,1:T(8,128)(2,1)S(1)} %copy.339), channel_id=1, source_target_pairs={{0,8},{8,16},{16,24},{24,32},{32,40},{40,48},{48,56},{56,64},{64,7... | collective-permute-start | bytes 98312 | tf_op jit(solution)/shard_map/while/body/eval_jaxpr/ppermute | solution.py:18
  1826.3 27.2 %collective-permute-start = (bf16[128,1,128]{2,0,1:T(8,128)(2,1)S(1)}, bf16[128,1,128]{2,0,1:T(8,128)(2,1)S(1)}, u32[]{:S(2)}, u32[]{:S(2)}) collective-permute-start(bf16[128,1,128]{2,0,1:T(8,128)(2,1)S(1)} %copy.339), channel_id=1, source_target_pairs={{0,8},{8,16},{16,24},{24,32},{32,40},{40,48},{48,56},{56,64},{64,7... | collective-permute-start | bytes 98312 | tf_op jit(solution)/shard_map/while/body/eval_jaxpr/ppermute | solution.py:18
  1858.2 26.2 %collective-permute-start = (bf16[128,1,128]{2,0,1:T(8,128)(2,1)S(1)}, bf16[128,1,128]{2,0,1:T(8,128)(2,1)S(1)}, u32[]{:S(2)}, u32[]{:S(2)}) collective-permute-start(bf16[128,1,128]{2,0,1:T(8,128)(2,1)S(1)} %copy.339), channel_id=1, source_target_pairs={{0,8},{8,16},{16,24},{24,32},{32,40},{40,48},{48,56},{56,64},{64,7... | collective-permute-start | bytes 98312 | tf_op jit(solution)/shard_map/while/body/eval_jaxpr/ppermute | solution.py:18
  2002.0 29.5 %collective-permute-start = (bf16[128,1,128]{2,0,1:T(8,128)(2,1)S(1)}, bf16[128,1,128]{2,0,1:T(8,128)(2,1)S(1)}, u32[]{:S(2)}, u32[]{:S(2)}) collective-permute-start(bf16[128,1,128]{2,0,1:T(8,128)(2,1)S(1)} %copy.339), channel_id=1, source_target_pairs={{0,8},{8,16},{16,24},{24,32},{32,40},{40,48},{48,56},{56,64},{64,7... | collective-permute-start | bytes 98312 | tf_op jit(solution)/shard_map/while/body/eval_jaxpr/ppermute | solution.py:18
  2117.0 27.1 %collective-permute-start = (bf16[128,1,128]{2,0,1:T(8,128)(2,1)S(1)}, bf16[128,1,128]{2,0,1:T(8,128)(2,1)S(1)}, u32[]{:S(2)}, u32[]{:S(2)}) collective-permute-start(bf16[128,1,128]{2,0,1:T(8,128)(2,1)S(1)} %copy.339), channel_id=1, source_target_pairs={{0,8},{8,16},{16,24},{24,32},{32,40},{40,48},{48,56},{56,64},{64,7... | collective-permute-start | bytes 98312 | tf_op jit(solution)/shard_map/while/body/eval_jaxpr/ppermute | solution.py:18
  2146.0 27.1 %collective-permute-start = (bf16[128,1,128]{2,0,1:T(8,128)(2,1)S(1)}, bf16[128,1,128]{2,0,1:T(8,128)(2,1)S(1)}, u32[]{:S(2)}, u32[]{:S(2)}) collective-permute-start(bf16[128,1,128]{2,0,1:T(8,128)(2,1)S(1)} %copy.339), channel_id=1, source_target_pairs={{0,8},{8,16},{16,24},{24,32},{32,40},{40,48},{48,56},{56,64},{64,7... | collective-permute-start | bytes 98312 | tf_op jit(solution)/shard_map/while/body/eval_jaxpr/ppermute | solution.py:18
  2188.7 25.9 %all-to-all-start.5 = ((bf16[64,128,2]{1,2,0:T(2,128)(2,1)}), bf16[64,128,2]{1,2,0:T(2,128)(2,1)S(1)}, u32[]{:S(2)}, u32[]{:S(2)}) async-start(bf16[64,128,2]{1,2,0:T(2,128)(2,1)} %fusion.174), calls=%async_computation.5 | async-start | bytes 65536 | tf_op jit(solution)/shard_map/all_to_all | solution.py:222
  (247 other events, 4027.3 us)
Sparse Core Ops, SparseCore 0:
  13.1 142.2 all-gather.2
  160.5 132.2 all-gather.4
where the time goes:
time: 2250 us; the launch traced here: 2240 us
  starting transfers between devices  1470 us (65%)
  waiting for transfers between devices  498 us (22%)
  local copies, waits for them, and re-layouts  147 us (7%)
  matrix products  80.5 us (4%)
    ppermute x256, starting transfers between devices, passed_along(): return lax.ppermute(value, axis, pairs)  1410 us
    ppermute x256, waiting for transfers between devices, passed_along(): return lax.ppermute(value, axis, pairs)  312 us
    all_gather x1, waiting for transfers between devices, per_device(): lax.all_gather(values, 'ctx', axis=0, tiled=True)  133 us
    gather x66, local copies, waits for them, and re-layouts, stored_positions(): return jnp.take(block_order, rows // half) * half + rows % half  129 us
  transfers between devices with their start and end apart: 264, of which 116 were waited for; matrix products, arithmetic and copies ran while one was open for 10% of the time, Pallas kernels for 0%

commit v1 on v0

v1 whole, which is shorter than its diff:
```python
import math

import jax
import jax.numpy as jnp
from jax import lax
from jax.experimental import pallas as pl
from jax.experimental.pallas import tpu as pltpu
from jax.sharding import PartitionSpec as P

T = 128
HALF = 64
N = 8
SEQ = T * N * N
WIDTH = 1024
LOG2E = 1.4426950408889634
HIDDEN = -1e30
MESH = pl.DeviceIdType.MESH
F32 = jnp.float32
BF16 = jnp.bfloat16


def nn(a, b):
    return lax.dot_general(a, b, (((1,), (0,)), ((), ())), preferred_element_type=F32)


def nt(a, b):
    return lax.dot_general(a, b, (((1,), (1,)), ((), ())), preferred_element_type=F32)


def iota(shape, dim):
    return lax.broadcasted_iota(jnp.int32, shape, dim)


def one_hot(cond):
    return jnp.where(cond, 1.0, 0.0).astype(BF16)


def flip(x):
    return x.astype(F32).T


def row_source(r):
    return (r & 7) * N + (r >> 4)


def row_channel(r):
    return (r >> 3) & 1


def to_rows():
    out, inn = iota((T, T), 0), iota((T, T), 1)
    return one_hot(inn == (out & 7) * 16 + (out >> 4) * 2 + ((out >> 3) & 1))


def from_rows():
    inn, out = iota((T, T), 1), iota((T, T), 0)
    return one_hot(out == (inn & 7) * 16 + (inn >> 4) * 2 + ((inn >> 3) & 1))


def toeplitz(chunks, table, first):
    ahead = iota((HALF, T), 1) >= iota((HALF, T), 0)

    def step(n, before):
        line = jnp.broadcast_to(chunks[pl.ds(n, 1), :], (HALF, T))
        now = pltpu.roll(line, 0, 1, stride=1, stride_axis=0)
        table[pl.ds(first, HALF), pl.ds(pl.multiple_of(n * T, T), T)] = jnp.where(
            ahead, now, before
        ).astype(BF16)
        return now

    lax.fori_loop(0, SEQ // T, step, jnp.zeros((HALF, T), F32), unroll=4)


def long_product(table, rows, blocks):
    lane = iota((HALF, T), 1)

    def step(g, total):
        parts = []
        for u in range(4):
            d = g * 4 + u
            moved = pltpu.roll(blocks, d, 1)
            parts.append(jnp.where(lane >= d, moved, 0.0).astype(BF16))
        right = jnp.concatenate(parts, axis=0)
        left = table[pl.ds(0, rows), pl.ds(pl.multiple_of(g * 256, 256), 256)]
        return total + nn(left, right)

    return lax.fori_loop(0, T // 4, step, jnp.zeros((rows, T), F32), unroll=4)


def kernel(
    order_s, order_v, q_ref, k_ref, v_ref, hq_ref, hv_ref, taps_ref, gain_ref, up_ref,
    dq_out, dk_out, dv_out, dhq_out, dhv_out, dtaps_out,
    q_all, k_all, v_all, vt, kt, scores,
    tg1_s, tg1, tg2_s, tg2, o_s, o_r, os_s, os_r, bm1_s, bm1, bm2_s, bm2,
    st_s, st_r, do_s, do_r, ds_s, ds_r, mx1_s, mx1, mx2_s, mx2,
    cg1_s, cg1, cg2_s, cg2, dq_s, dq_r, dkv_s, dkv_r,
    up_t, hv_t, hvg_t, gain_t, table, chunks, dk_acc, dv_acc,
    send, recv,
):
    me = lax.axis_index("ctx")
    head = lax.axis_index("ch")
    y = lax.div(me, N)
    c = lax.rem(me, N)
    scale = 1.0 / math.sqrt(T)
    tap_scale = SEQ ** (-0.5)

    def y_peer(k):
        p = lax.rem(y + k, N)
        return p, (p * N + c, head)

    def c_peer(k):
        p = lax.rem(c + k, N)
        return p, (y * N + p, head)

    def h_peer(k):
        p = lax.rem(head + k, N)
        return p, (me, p)

    def spread(peer, src, dst, slot, sem):
        def step(k, _):
            p, device = peer(k)
            pltpu.make_async_remote_copy(
                src_ref=src(p),
                dst_ref=dst.at[slot],
                send_sem=send.at[sem],
                recv_sem=recv.at[sem],
                device_id=device,
                device_id_type=MESH,
            ).start()
            return 0

        lax.fori_loop(1, N, step, 0)

    def arrived(dst, sem):
        part = dst.at[pl.ds(0, N - 1)]
        pltpu.make_async_copy(part, part, recv.at[sem]).wait()

    def left(dst, sem):
        part = dst.at[pl.ds(0, N - 1)]
        pltpu.make_async_copy(part, part, send.at[sem]).wait()

    barrier = pltpu.get_barrier_semaphore()

    def greet(k, _):
        for peer in (y_peer, c_peer, h_peer):
            pl.semaphore_signal(barrier, inc=1, device_id=peer(k)[1], device_id_type=MESH)
        return 0

    lax.fori_loop(1, N, greet, 0)

    up = up_ref[...].astype(F32)
    gated = (up * hq_ref[...].astype(F32)).astype(BF16)
    tg1_s[:, 0:16, :] = flip(gated).astype(BF16).reshape(N, 16, T)
    tg1_s[:, 16:32, :] = flip(taps_ref[...]).astype(BF16).reshape(N, 16, T)
    tg1[y] = tg1_s[y]
    q_all[y] = q_ref[...]
    k_all[c] = k_ref[...]
    v_all[c] = v_ref[...]
    pl.semaphore_wait(barrier, 3 * (N - 1))

    spread(y_peer, lambda p: tg1_s.at[p], tg1, y, 0)
    spread(c_peer, lambda p: k_ref, k_all, c, 1)
    spread(y_peer, lambda p: q_ref, q_all, y, 2)
    spread(c_peer, lambda p: v_ref, v_all, c, 3)

    up_t[...] = flip(up)
    hv_t[...] = flip(hv_ref[...])
    gain_t[...] = jnp.broadcast_to(gain_ref[...], (T, T)).T
    hvg_t[...] = hv_t[...] * gain_t[...]

    row = iota((T, T), 1)
    line = iota((T, T), 0)
    order = jnp.broadcast_to(order_v[...].astype(F32), (8, T)).astype(BF16)
    place = [
        nn(order, one_hot(line == row_source(row) * 2 + h))[0:1, :].astype(jnp.int32) for h in (0, 1)
    ]
    ours = [row_channel(row) == j for j in (0, 1)]

    def forward(j, h):
        return one_hot(ours[j] & (place[h] == line))

    def backward(j, h):
        return one_hot(ours[j] & (place[h] == T - 1 - line))

    def lag_order(j, h):
        return one_hot(ours[j] & (row_source(row) * 2 + h == T - 1 - line))

    arrived(tg1, 0)
    order_in = to_rows()
    for lo in (0, 16):
        tg2_s[:, lo : lo + 16, :] = (
            nn(order_in, tg1[:, lo : lo + 16, :].reshape(T, T)).astype(BF16).reshape(N, 16, T)
        )
    tg2[c] = tg2_s[c]
    spread(c_peer, lambda p: tg2_s.at[p], tg2, c, 4)
    arrived(tg2, 4)

    grads = tg2[:, 0:16, :].reshape(T, T)
    taps = tg2[:, 16:32, :].reshape(T, T)
    grads_t = flip(grads).astype(BF16)
    narrow_row, narrow_line = iota((HALF, T), 1), iota((HALF, T), 0)
    back_t = [jnp.zeros((HALF, T), F32)] * 2
    for j in (0, 1):
        mine = row_channel(narrow_row) == j
        chunks[j] = nn(one_hot(mine & (row_source(narrow_row) == narrow_line)), taps)
        toeplitz(chunks.at[j], table.at[j], 0)
        blocks = nt(grads_t[0:HALF], backward(j, 0)) + nt(grads_t[HALF:T], backward(j, 1))
        result = (long_product(table.at[j], HALF, blocks) * tap_scale).astype(BF16)
        for h in (0, 1):
            back_t[h] = back_t[h] + nn(result, backward(j, h))
    bm1_s[...] = flip(jnp.concatenate(back_t, axis=0)).astype(BF16).reshape(N, 16, T)
    bm1[c] = bm1_s[c]
    spread(c_peer, lambda p: bm1_s.at[p], bm1, c, 5)

    arrived(k_all, 1)
    arrived(q_all, 2)
    arrived(v_all, 3)
    for i in range(N):
        vt[:, i * T : (i + 1) * T] = flip(v_all[i]).astype(BF16)
        kt[:, i * T : (i + 1) * T] = flip(k_all[i]).astype(BF16)

    within = iota((1, 2 * T), 1)
    deep = iota((HALF, 2 * T), 0)

    def query_places(pair):
        base = within & (HALF - 1)
        spot = jnp.zeros((1, 2 * T), jnp.int32)
        for e in range(4):
            block = order_s[((pair * 2 + e // 2) * N + c) * 2 + e % 2]
            spot = jnp.where((within >> 6) == e, block * HALF, spot)
        return spot + base

    def masked(tile, pair_q, spots):
        keys = k_all[2 * tile : 2 * tile + 2].reshape(2 * T, T)
        raw = nt(keys, pair_q) * (scale * LOG2E)
        out = []
        for e in range(4):
            block = order_s[y * 16 + tile * 4 + e]
            out.append(
                jnp.where(deep <= spots - block * HALF, raw[e * HALF : (e + 1) * HALF], HIDDEN)
            )
        return jnp.concatenate(out, axis=0)

    def attend(pair, _):
        pair_q = q_all[pl.ds(pair * 2, 2)].reshape(2 * T, T)
        spots = query_places(pair)
        peak = jnp.full((1, 2 * T), HIDDEN, F32)
        for tile in range(4):
            part = masked(tile, pair_q, spots)
            scores[tile * 256 : (tile + 1) * 256, :] = part
            peak = jnp.maximum(peak, jnp.max(part, axis=0, keepdims=True))
        total = jnp.zeros((1, 2 * T), F32)
        out = jnp.zeros((T, 2 * T), F32)
        for tile in range(4):
            weights = jnp.exp2(scores[tile * 256 : (tile + 1) * 256, :] - peak)
            total = total + jnp.sum(weights, axis=0, keepdims=True)
            out = out + nn(vt[:, tile * 256 : (tile + 1) * 256], weights.astype(BF16))
        for e in (0, 1):
            lanes = slice(e * T, (e + 1) * T)
            o_s[pair * 2 + e] = out[:, lanes].astype(BF16)
            os_s[pair * 2 + e] = jnp.concatenate([peak[:, lanes], total[:, lanes]], axis=0)
        return 0

    lax.fori_loop(0, 4, attend, 0)
    o_r[y] = o_s[y]
    os_r[y] = os_s[y]
    spread(y_peer, lambda p: os_s.at[p], os_r, y, 6)
    spread(y_peer, lambda p: o_s.at[p], o_r, y, 7)

    arrived(bm1, 5)
    order_out = from_rows()
    bm2_s[...] = nn(order_out, bm1[...].reshape(T, T)).astype(BF16).reshape(N, 16, T)
    bm2[y] = bm2_s[y]
    spread(y_peer, lambda p: bm2_s.at[p], bm2, y, 8)

    for j in (0, 1):
        mine = row_channel(narrow_row) == j
        flat = jnp.zeros((HALF, T), F32)
        for h in (0, 1):
            for hh in (0, 1):
                turn = one_hot(
                    ((row >> 6) == hh) & (line == h * HALF + HALF - 1 - (row & (HALF - 1)))
                )
                pick = one_hot(mine & (place[h] == T - 1 - 2 * narrow_line - hh))
                flat = flat + nn(pick, nn(grads, turn).astype(BF16))
        chunks[j] = flat
        toeplitz(chunks.at[j], table.at[j], HALF)

    arrived(os_r, 6)
    arrived(o_r, 7)
    peak = os_r[0, 0:1, :]
    for i in range(1, N):
        peak = jnp.maximum(peak, os_r[i, 0:1, :])
    total = jnp.zeros((1, T), F32)
    mix = jnp.zeros((T, T), F32)
    for i in range(N):
        factor = jnp.exp2(os_r[i, 0:1, :] - peak)
        total = total + factor * os_r[i, 1:2, :]
        mix = mix + factor * o_r[i].astype(F32)
    lse = peak + jnp.log2(total)
    act = (mix / total).astype(BF16).astype(F32)
    arrived(bm2, 8)
    back = bm2[...].reshape(T, T).astype(F32)
    scaled = back * hvg_t[...]
    st_s[...] = jnp.concatenate(
        [jnp.sum(act * act, axis=0, keepdims=True), jnp.sum(scaled * act, axis=0, keepdims=True)],
        axis=0,
    )
    st_r[head] = st_s[...]
    spread(h_peer, lambda p: st_s, st_r, head, 9)
    arrived(st_r, 9)
    sums = st_r[0]
    for i in range(1, N):
        sums = sums + st_r[i]
    inv_root = lax.rsqrt(sums[0:1, :] / WIDTH + 1e-06)
    inner = sums[1:2, :]
    grad_att = (inv_root * scaled - act * (inv_root * inv_root * inv_root) * (inner / WIDTH)).astype(BF16)
    do_s[...] = grad_att
    do_r[y] = grad_att
    spread(y_peer, lambda p: do_s, do_r, y, 10)
    delta = jnp.sum(grad_att.astype(F32) * act, axis=0, keepdims=True)
    ds_s[...] = jnp.concatenate([lse, delta], axis=0)
    ds_r[y] = ds_s[...]
    spread(y_peer, lambda p: ds_s, ds_r, y, 11)
    normed = act * inv_root * gain_t[...]
    mx1_s[...] = (normed * hv_t[...]).astype(BF16).reshape(N, 16, T)
    mx1[y] = mx1_s[y]
    spread(y_peer, lambda p: mx1_s.at[p], mx1, y, 12)
    dhv_out[...] = flip((back * normed).astype(BF16)).astype(BF16)

    arrived(mx1, 12)
    mx2_s[...] = nn(order_in, mx1[...].reshape(T, T)).astype(BF16).reshape(N, 16, T)
    mx2[c] = mx2_s[c]
    spread(c_peer, lambda p: mx2_s.at[p], mx2, c, 13)

    dk_acc[...] = jnp.zeros((N * T, T), F32)
    dv_acc[...] = jnp.zeros((N * T, T), F32)
    arrived(do_r, 10)
    arrived(ds_r, 11)

    def grad(pair, _):
        pair_q = q_all[pl.ds(pair * 2, 2)].reshape(2 * T, T)
        spots = query_places(pair)
        low, high = do_r[pair * 2], do_r[pair * 2 + 1]
        pair_do = jnp.concatenate([low, high], axis=1)
        both = jnp.concatenate([ds_r[pair * 2], ds_r[pair * 2 + 1]], axis=1)
        dq = jnp.zeros((T, 2 * T), F32)
        for tile in range(4):
            rows = slice(tile * 256, (tile + 1) * 256)
            probs = jnp.exp2(masked(tile, pair_q, spots) - both[0:1, :])
            dprobs = nn(v_all[2 * tile : 2 * tile + 2].reshape(2 * T, T), pair_do)
            dscores = (probs * (dprobs - both[1:2, :])).astype(BF16)
            dv_acc[rows, :] += nt(probs.astype(BF16), pair_do)
            dk_acc[rows, :] += nn(dscores, pair_q)
            dq = dq + nn(kt[:, rows], dscores)
        for e in (0, 1):
            dq_s[pair * 2 + e] = (dq[:, e * T : (e + 1) * T] * scale).astype(BF16)
        return 0

    lax.fori_loop(0, 4, grad, 0)
    dkv_s[:, 0:T, :] = (dk_acc[...] * scale).astype(BF16).reshape(N, T, T)
    dkv_s[:, T : 2 * T, :] = dv_acc[...].astype(BF16).reshape(N, T, T)
    spread(c_peer, lambda p: dkv_s.at[p], dkv_r, c, 14)
    dkv_r[c] = dkv_s[c]
    spread(y_peer, lambda p: dq_s.at[p], dq_r, y, 15)
    dq_r[y] = dq_s[y]

    arrived(mx2, 13)
    within_half = one_hot(line == (row >> 6) * HALF + HALF - 1 - (row & (HALF - 1)))
    turned_t = flip(nn(mx2[...].reshape(T, T), within_half)).astype(BF16)
    conv_t = [jnp.zeros((HALF, T), F32)] * 2
    lags_t = [jnp.zeros((HALF, T), F32)] * 2
    for j in (0, 1):
        blocks = nt(turned_t[0:HALF], forward(j, 0)) + nt(turned_t[HALF:T], forward(j, 1))
        result = (long_product(table.at[j], T, blocks) * tap_scale).astype(BF16)
        for h in (0, 1):
            conv_t[h] = conv_t[h] + nn(result[0:HALF], forward(j, h))
            lags_t[h] = lags_t[h] + nn(result[HALF:T], lag_order(j, h))
    conv_rows = nn(flip(jnp.concatenate(conv_t, axis=0)).astype(BF16), within_half)
    cg1_s[:, 0:16, :] = conv_rows.astype(BF16).reshape(N, 16, T)
    cg1_s[:, 16:32, :] = flip(jnp.concatenate(lags_t, axis=0)).astype(BF16).reshape(N, 16, T)
    cg1[c] = cg1_s[c]
    spread(c_peer, lambda p: cg1_s.at[p], cg1, c, 16)
    arrived(cg1, 16)
    for lo in (0, 16):
        cg2_s[:, lo : lo + 16, :] = (
            nn(order_out, cg1[:, lo : lo + 16, :].reshape(T, T)).astype(BF16).reshape(N, 16, T)
        )
    cg2[y] = cg2_s[y]
    spread(y_peer, lambda p: cg2_s.at[p], cg2, y, 17)

    arrived(dq_r, 15)
    grad_q = dq_r[0].astype(F32)
    for i in range(1, N):
        grad_q = grad_q + dq_r[i].astype(F32)
    dq_out[...] = grad_q.T.astype(BF16)
    arrived(dkv_r, 14)
    grad_kv = dkv_r[0].astype(F32)
    for i in range(1, N):
        grad_kv = grad_kv + dkv_r[i].astype(F32)
    dk_out[...] = grad_kv[0:T].astype(BF16)
    dv_out[...] = grad_kv[T : 2 * T].astype(BF16)

    arrived(cg2, 17)
    dhq_out[...] = flip(up_t[...] * cg2[:, 0:16, :].reshape(T, T).astype(F32)).astype(BF16)
    dtaps_out[...] = flip(cg2[:, 16:32, :].reshape(T, T)).astype(BF16)

    for sem, dst in enumerate(
        (tg1, k_all, q_all, v_all, tg2, bm1, os_r, o_r, bm2, st_r, do_r, ds_r, mx1, mx2, dkv_r, dq_r, cg1, cg2)
    ):
        left(dst, sem)


def per_device(queries, keys_in, values, hq, hv, taps, gain, upstream, order):
    def vmem(*shape, dtype=BF16):
        return pltpu.VMEM(shape, dtype)

    pair16 = vmem(N, 16, T)
    pair32 = vmem(N, 32, T)
    square = vmem(N, T, T)
    tall = vmem(N, 2 * T, T)
    lines = vmem(N, 2, T, dtype=F32)
    wide = vmem(T, T, dtype=F32)
    in_vmem = pl.BlockSpec(memory_space=pltpu.VMEM)
    out = jax.ShapeDtypeStruct((T, T), BF16)
    return pl.pallas_call(
        kernel,
        out_shape=(out,) * 6,
        in_specs=[pl.BlockSpec(memory_space=pltpu.SMEM)] + [in_vmem] * 9,
        out_specs=(in_vmem,) * 6,
        scratch_shapes=[
            square, square, square, vmem(T, N * T), vmem(T, N * T), vmem(N * T, 2 * T, dtype=F32),
            pair32, pair32, pair32, pair32, square, square, lines, lines, pair16, pair16, pair16, pair16,
            vmem(2, T, dtype=F32), lines, vmem(T, T), square, vmem(2, T, dtype=F32), lines,
            pair16, pair16, pair16, pair16,
            pair32, pair32, pair32, pair32, square, square, tall, tall,
            wide, wide, wide, wide, vmem(2, T, SEQ), vmem(2, HALF, T, dtype=F32),
            vmem(N * T, T, dtype=F32), vmem(N * T, T, dtype=F32),
            pltpu.SemaphoreType.DMA((18,)), pltpu.SemaphoreType.DMA((18,)),
        ],
        compiler_params=pltpu.CompilerParams(
            collective_id=0, has_side_effects=True, vmem_limit_bytes=48 * 1024 * 1024
        ),
        name="pair_backward",
    )(order, order.reshape(1, -1), queries, keys_in, values, hq, hv, taps, gain.reshape(1, -1), upstream)


def solution(mesh):
    rows = P("ctx", "ch")
    return jax.shard_map(
        per_device,
        mesh=mesh,
        in_specs=(rows,) * 6 + (P("ch"), rows, P()),
        out_specs=(rows,) * 6,
        check_vma=False,
    )
```

time: 2250 us -> 104 us (0.05)
  the two profiles are of different devices: /device:TPU:70 before, /device:TPU:1 now
where the time goes in v1:
time: 104 us; the launch traced here: 103 us
  Pallas kernels  92.9 us (89%)
  local copies, waits for them, and re-layouts  9.65 us (9%)
    pallas_call x1, Pallas kernels, per_device(): pl.pallas_call(kernel, out_shape=(out,) * 6, in_specs=[pl.BlockSpec(memor...  92.9 us
    unnamed x24, local copies, waits for them, and re-layouts  9.65 us

profile of v1, /device:TPU:1, one launch (start us, length us, event | category | flops | bytes accessed | tf_op | source)
XLA Modules:
  0.0 103.2 jit_solution(18281652113627634315)
XLA Ops:
  0.6 0.0 copy-start.7
  0.6 0.0 copy-start.8
  0.7 0.6 copy-done.7
  1.3 0.0 copy-done.8
  1.3 0.0 copy-start
  1.3 0.8 copy-done
  2.1 0.0 copy-start.1
  2.1 0.8 copy-done.1
  2.8 0.0 copy-start.2
  2.8 0.8 copy-done.2
  3.6 0.0 copy-start.3
  3.6 0.8 copy-done.3
  4.3 0.0 copy-start.4
  4.3 0.8 copy-done.4
  5.1 0.0 copy-start.5
  5.1 0.8 copy-done.5
  5.9 0.8 copy-done.6
  6.6 92.9 %pair_backward.1 = (bf16[128,128]{1,0:T(8,128)(2,1)S(1)}, bf16[128,128]{1,0:T(8,128)(2,1)S(1)}, bf16[128,128]{1,0:T(8,128)(2,1)S(1)}, bf16[128,128]{1,0:T(8,128)...) custom-call(s32[128]{0:T(128)S(1)} %copy-done.7, s32[1,128]{1,0:T(1,128)S(1)} %bitcast.2, ...), custom_call_target="tpu_custom_call" | custom-call | tf_op jit(solution)/shard_map/pair_backward/pallas_call | solution.py:426
  99.5 0.6 copy.21
  100.2 0.6 copy.22
  100.8 0.6 copy.23
  101.4 0.6 copy.24
  102.0 0.6 copy.25
  102.6 0.6 copy.26
  (1 shorter events, 0.0 us)
Async XLA Ops:
  0.6 0.7 copy-start.7
  0.6 0.7 copy-start.8
  1.3 0.8 copy-start
  2.1 0.8 copy-start.1
  2.8 0.8 copy-start.2
  3.6 0.8 copy-start.3
  4.3 0.8 copy-start.4
  5.1 0.8 copy-start.5
  5.9 0.8 copy-start.6

commit v2 on v1

v2 whole, which is shorter than its diff:
```python
import math

import jax
import jax.numpy as jnp
from jax import lax
from jax.experimental import pallas as pl
from jax.experimental.pallas import tpu as pltpu
from jax.sharding import PartitionSpec as P

T = 128
HALF = 64
N = 8
SEQ = T * N * N
WIDTH = 1024
LOG2E = 1.4426950408889634
HIDDEN = -1e30
MESH = pl.DeviceIdType.MESH
F32 = jnp.float32
BF16 = jnp.bfloat16


def nn(a, b):
    return lax.dot_general(a, b, (((1,), (0,)), ((), ())), preferred_element_type=F32)


def nt(a, b):
    return lax.dot_general(a, b, (((1,), (1,)), ((), ())), preferred_element_type=F32)


def iota(shape, dim):
    return lax.broadcasted_iota(jnp.int32, shape, dim)


def one_hot(cond):
    return jnp.where(cond, 1.0, 0.0).astype(BF16)


def flip(x):
    return x.astype(F32).T


def row_source(r):
    return (r & 7) * N + (r >> 4)


def row_channel(r):
    return (r >> 3) & 1


def to_rows():
    out, inn = iota((T, T), 0), iota((T, T), 1)
    return one_hot(inn == (out & 7) * 16 + (out >> 4) * 2 + ((out >> 3) & 1))


def from_rows():
    inn, out = iota((T, T), 1), iota((T, T), 0)
    return one_hot(out == (inn & 7) * 16 + (inn >> 4) * 2 + ((inn >> 3) & 1))


def toeplitz(chunks, table, first):
    ahead = iota((HALF, T), 1) >= iota((HALF, T), 0)

    def step(n, before):
        after = []
        for j in (0, 1):
            line = jnp.broadcast_to(chunks[j, pl.ds(n, 1), :], (HALF, T))
            now = pltpu.roll(line, 0, 1, stride=1, stride_axis=0)
            table[j, pl.ds(first, HALF), pl.ds(pl.multiple_of(n * T, T), T)] = jnp.where(
                ahead, now, before[j]
            ).astype(BF16)
            after.append(now)
        return tuple(after)

    empty = jnp.zeros((HALF, T), F32)
    lax.fori_loop(0, SEQ // T, step, (empty, empty), unroll=4)


def long_products(table, steps, wide):
    totals = [jnp.zeros((T, wide), F32)] * 2
    for part in range(4):
        top = part * 32
        rows = T - top

        def step(g, sums):
            p = part * 8 + g
            out = []
            for j in (0, 1):
                pair = [
                    steps[j, pl.ds(T + top - 4 * p - 2 * u, rows), :].astype(BF16) for u in (0, 1)
                ]
                right = table[j, 0:wide, pl.ds(pl.multiple_of(p * 256, 256), 256)]
                out.append(sums[j] + nt(jnp.concatenate(pair, axis=1), right))
            return tuple(out)

        sums = lax.fori_loop(0, 8, step, tuple(t[top:] for t in totals), unroll=2)
        if top:
            sums = [jnp.concatenate([totals[j][0:top], sums[j]], axis=0) for j in (0, 1)]
        totals = list(sums)
    return totals


def kernel(
    order_h, q_h, k_h, v_h, hq_h, hv_h, taps_h, gain_h, up_h,
    packed,
    order_s, order_v, hq_ref, hv_ref, taps_ref, gain_ref, up_ref,
    q_all, k_all, v_all, vt, kt, scores,
    tg1_s, tg1, tg2_s, tg2, o_s, o_r, os_s, os_r, bm1_s, bm1, bm2_s, bm2,
    ss_s, ss_r, in_s, in_r, do_s, do_r, ds_s, ds_r, mx1_s, mx1, mx2_s, mx2,
    cg1_s, cg1, cg2_s, cg2, dq_s, dq_r, dkv_s, dkv_r,
    up_t, hv_t, hvg_t, gain_t, table, chunks, steps, dk_acc, dv_acc,
    send, recv, load,
):
    me = lax.axis_index("ctx")
    head = lax.axis_index("ch")
    y = lax.div(me, N)
    c = lax.rem(me, N)
    scale = 1.0 / math.sqrt(T)
    tap_scale = SEQ ** (-0.5)

    def y_peer(k):
        p = lax.rem(y + k, N)
        return p, (p * N + c, head)

    def c_peer(k):
        p = lax.rem(c + k, N)
        return p, (y * N + p, head)

    def h_peer(k):
        p = lax.rem(head + k, N)
        return p, (me, p)

    started = []

    def spread(peer, src, dst, slot):
        sem = len(started)
        started.append(dst)

        def step(k, _):
            p, device = peer(k)
            pltpu.make_async_remote_copy(
                src_ref=src(p),
                dst_ref=dst.at[slot],
                send_sem=send.at[sem],
                recv_sem=recv.at[sem],
                device_id=device,
                device_id_type=MESH,
            ).start()
            return 0

        lax.fori_loop(1, N, step, 0)

        def arrived():
            part = dst.at[pl.ds(0, N - 1)]
            pltpu.make_async_copy(part, part, recv.at[sem]).wait()

        return arrived

    barrier = pltpu.get_barrier_semaphore()

    def greet(k, _):
        for peer in (y_peer, c_peer, h_peer):
            pl.semaphore_signal(barrier, inc=1, device_id=peer(k)[1], device_id_type=MESH)
        return 0

    lax.fori_loop(1, N, greet, 0)

    loads = [
        pltpu.make_async_copy(src, dst, load.at[i])
        for i, (src, dst) in enumerate(
            (
                (up_h, up_ref), (hq_h, hq_ref), (taps_h, taps_ref), (q_h, q_all.at[y]), (k_h, k_all.at[c]),
                (v_h, v_all.at[c]), (hv_h, hv_ref), (gain_h, gain_ref), (order_h, order_s), (order_h, order_v),
            )
        )
    ]
    for each in loads:
        each.start()
    for each in loads[0:3]:
        each.wait()
    up = up_ref[...].astype(F32)
    gated = (up * hq_ref[...].astype(F32)).astype(BF16)
    tg1_s[:, 0:16, :] = flip(gated).astype(BF16).reshape(N, 16, T)
    tg1_s[:, 16:32, :] = flip(taps_ref[...]).astype(BF16).reshape(N, 16, T)
    tg1[y] = tg1_s[y]
    for each in loads[3:]:
        each.wait()
    pl.semaphore_wait(barrier, 3 * (N - 1))

    tg1_here = spread(y_peer, lambda p: tg1_s.at[p], tg1, y)
    k_here = spread(c_peer, lambda p: k_all.at[c], k_all, c)
    q_here = spread(y_peer, lambda p: q_all.at[y], q_all, y)
    v_here = spread(c_peer, lambda p: v_all.at[c], v_all, c)

    up_t[...] = flip(up)
    hv_t[...] = flip(hv_ref[...])
    gain_t[...] = jnp.broadcast_to(gain_ref[...], (T, T)).T
    hvg_t[...] = hv_t[...] * gain_t[...]
    steps[:, 0:T, :] = jnp.zeros((2, T, T), F32)
    dk_acc[...] = jnp.zeros((N * T, T), F32)
    dv_acc[...] = jnp.zeros((N * T, T), F32)

    lane = iota((T, T), 1)
    line = iota((T, T), 0)
    order = jnp.broadcast_to(order_v[...].astype(F32), (8, T)).astype(BF16)
    place_f = [nn(order, one_hot(line == row_source(lane) * 2 + h))[0:1, :] for h in (0, 1)]
    place = [p.astype(jnp.int32) for p in place_f]
    place_t = [jnp.broadcast_to(p, (T, T)).T.astype(jnp.int32) for p in place_f]
    ours = [row_channel(lane) == j for j in (0, 1)]
    ours_t = [row_channel(line) == j for j in (0, 1)]
    here = lane & (HALF - 1)

    def lay_out(rows, turned, reverse):
        moved = [
            nn(rows, one_hot((line == h * HALF + (HALF - 1 - here if turned else here)) & ((lane >> 6) == e))).astype(BF16)
            for h in (0, 1)
            for e in (0, 1)
        ]
        for j in (0, 1):
            total = jnp.zeros((T, T), F32)
            for h in (0, 1):
                for e in (0, 1):
                    want = T - 1 - line + e if reverse else line - e
                    total = total + nn(one_hot(ours[j] & (place[h] == want)), moved[h * 2 + e])
            steps[j, T : 2 * T, :] = total

    def collect(results, spot, first, turned):
        total = jnp.zeros((T, T), F32)
        for h in (0, 1):
            mine = jnp.zeros((T, results[0].shape[1]), F32)
            for j in (0, 1):
                mine = mine + nn(one_hot(ours_t[j] & (spot[h] == lane)), results[j])
            wide = results[0].shape[1]
            a, b = iota((wide, T), 0), iota((wide, T), 1)
            inside = b & (HALF - 1)
            put = (a == first + (HALF - 1 - inside if turned else inside)) & ((b >> 6) == h)
            total = total + nn(mine.astype(BF16), one_hot(put))
        return total.astype(BF16)

    within = iota((1, 2 * T), 1)
    deep = iota((HALF, 2 * T), 0)

    def query_places(pair):
        base = within & (HALF - 1)
        spot = jnp.zeros((1, 2 * T), jnp.int32)
        for e in range(4):
            block = order_s[0, ((pair * 2 + e // 2) * N + c) * 2 + e % 2]
            spot = jnp.where((within >> 6) == e, block * HALF, spot)
        return spot + base

    def masked(tile, pair_q, spots):
        keys = k_all[2 * tile : 2 * tile + 2].reshape(2 * T, T)
        raw = nt(keys, pair_q) * (scale * LOG2E)
        out = []
        for e in range(4):
            block = order_s[0, y * 16 + tile * 4 + e]
            out.append(
                jnp.where(deep <= spots - block * HALF, raw[e * HALF : (e + 1) * HALF], HIDDEN)
            )
        return jnp.concatenate(out, axis=0)

    def attend(pair, _):
        pair_q = q_all[pl.ds(pair * 2, 2)].reshape(2 * T, T)
        spots = query_places(pair)
        peak = jnp.full((1, 2 * T), HIDDEN, F32)
        for tile in range(4):
            part = masked(tile, pair_q, spots)
            scores[tile * 256 : (tile + 1) * 256, :] = part
            peak = jnp.maximum(peak, jnp.max(part, axis=0, keepdims=True))
        total = jnp.zeros((1, 2 * T), F32)
        out = jnp.zeros((T, 2 * T), F32)
        for tile in range(4):
            weights = jnp.exp2(scores[tile * 256 : (tile + 1) * 256, :] - peak)
            total = total + jnp.sum(weights, axis=0, keepdims=True)
            out = out + nn(vt[:, tile * 256 : (tile + 1) * 256], weights.astype(BF16))
        for e in (0, 1):
            lanes = slice(e * T, (e + 1) * T)
            o_s[pair * 2 + e] = out[:, lanes].astype(BF16)
            os_s[pair * 2 + e] = jnp.concatenate([peak[:, lanes], total[:, lanes]], axis=0)
        return 0

    def forward_part():
        k_here()
        q_here()
        v_here()
        for i in range(N):
            vt[:, i * T : (i + 1) * T] = flip(v_all[i]).astype(BF16)
            kt[:, i * T : (i + 1) * T] = flip(k_all[i]).astype(BF16)
        lax.fori_loop(0, 4, attend, 0)
        o_r[y] = o_s[y]
        os_r[y] = os_s[y]
        os_here = spread(y_peer, lambda p: os_s.at[p], os_r, y)
        o_here = spread(y_peer, lambda p: o_s.at[p], o_r, y)
        return os_here, o_here

    tg1_here()
    order_in = to_rows()
    order_out = from_rows()
    for lo in (0, 16):
        tg2_s[:, lo : lo + 16, :] = (
            nn(order_in, tg1[:, lo : lo + 16, :].reshape(T, T)).astype(BF16).reshape(N, 16, T)
        )
    tg2[c] = tg2_s[c]
    tg2_here = spread(c_peer, lambda p: tg2_s.at[p], tg2, c)

    os_here, o_here = forward_part()

    tg2_here()
    grads = tg2[:, 0:16, :].reshape(T, T)
    taps = tg2[:, 16:32, :].reshape(T, T)
    narrow_lane, narrow_line = iota((HALF, T), 1), iota((HALF, T), 0)
    narrow_ours = [row_channel(narrow_lane) == j for j in (0, 1)]
    for j in (0, 1):
        chunks[j] = nn(one_hot(narrow_ours[j] & (row_source(narrow_lane) == narrow_line)), taps)
    toeplitz(chunks, table, 0)
    lay_out(grads, False, True)
    backs = [(r * tap_scale).astype(BF16) for r in long_products(table, steps, HALF)]
    flipped_t = [T - 1 - p for p in place_t]
    bm1_s[...] = collect(backs, flipped_t, 0, False).reshape(N, 16, T)
    bm1[c] = bm1_s[c]
    bm1_here = spread(c_peer, lambda p: bm1_s.at[p], bm1, c)

    flats = [jnp.zeros((HALF, T), F32)] * 2
    for h in (0, 1):
        for hh in (0, 1):
            turn = one_hot(((lane >> 6) == hh) & (line == h * HALF + HALF - 1 - here))
            turned = nn(grads, turn).astype(BF16)
            for j in (0, 1):
                pick = one_hot(narrow_ours[j] & (place[h] == T - 1 - 2 * narrow_line - hh))
                flats[j] = flats[j] + nn(pick, turned)
    for j in (0, 1):
        chunks[j] = flats[j]
    toeplitz(chunks, table, HALF)

    os_here()
    o_here()
    peak = os_r[0, 0:1, :]
    for i in range(1, N):
        peak = jnp.maximum(peak, os_r[i, 0:1, :])
    total = jnp.zeros((1, T), F32)
    mix = jnp.zeros((T, T), F32)
    for i in range(N):
        factor = jnp.exp2(os_r[i, 0:1, :] - peak)
        total = total + factor * os_r[i, 1:2, :]
        mix = mix + factor * o_r[i].astype(F32)
    lse = peak + jnp.log2(total)
    act = (mix / total).astype(BF16).astype(F32)
    ss_s[...] = jnp.sum(act * act, axis=0, keepdims=True)
    ss_r[head] = ss_s[...]
    ss_here = spread(h_peer, lambda p: ss_s, ss_r, head)

    bm1_here()
    bm2_s[...] = nn(order_out, bm1[...].reshape(T, T)).astype(BF16).reshape(N, 16, T)
    bm2[y] = bm2_s[y]
    bm2_here = spread(y_peer, lambda p: bm2_s.at[p], bm2, y)

    ss_here()
    square = ss_r[0]
    for i in range(1, N):
        square = square + ss_r[i]
    inv_root = lax.rsqrt(square / WIDTH + 1e-06)
    normed = act * inv_root * gain_t[...]
    mx1_s[...] = (normed * hv_t[...]).astype(BF16).reshape(N, 16, T)
    mx1[y] = mx1_s[y]
    mx1_here = spread(y_peer, lambda p: mx1_s.at[p], mx1, y)

    bm2_here()
    back = bm2[...].reshape(T, T).astype(F32)
    scaled = back * hvg_t[...]
    in_s[...] = jnp.sum(scaled * act, axis=0, keepdims=True)
    in_r[head] = in_s[...]
    in_here = spread(h_peer, lambda p: in_s, in_r, head)
    packed[4] = flip((back * normed).astype(BF16)).astype(BF16)

    mx1_here()
    mx2_s[...] = nn(order_in, mx1[...].reshape(T, T)).astype(BF16).reshape(N, 16, T)
    mx2[c] = mx2_s[c]
    mx2_here = spread(c_peer, lambda p: mx2_s.at[p], mx2, c)

    in_here()
    inner = in_r[0]
    for i in range(1, N):
        inner = inner + in_r[i]
    grad_att = (
        inv_root * scaled - act * (inv_root * inv_root * inv_root) * (inner / WIDTH)
    ).astype(BF16)
    do_s[...] = grad_att
    do_r[y] = grad_att
    do_here = spread(y_peer, lambda p: do_s, do_r, y)
    delta = jnp.sum(grad_att.astype(F32) * act, axis=0, keepdims=True)
    ds_s[...] = jnp.concatenate([lse, delta], axis=0)
    ds_r[y] = ds_s[...]
    ds_here = spread(y_peer, lambda p: ds_s, ds_r, y)

    mx2_here()
    lay_out(mx2[...].reshape(T, T), True, False)
    lates = [(r * tap_scale).astype(BF16) for r in long_products(table, steps, T)]
    lag_t = [T - 1 - (row_source(line) * 2 + h) for h in (0, 1)]
    cg1_s[:, 0:16, :] = collect(lates, place_t, 0, True).reshape(N, 16, T)
    cg1_s[:, 16:32, :] = collect(lates, lag_t, HALF, False).reshape(N, 16, T)
    cg1[c] = cg1_s[c]
    cg1_here = spread(c_peer, lambda p: cg1_s.at[p], cg1, c)

    do_here()
    ds_here()

    def grad(pair, _):
        pair_q = q_all[pl.ds(pair * 2, 2)].reshape(2 * T, T)
        spots = query_places(pair)
        low, high = do_r[pair * 2], do_r[pair * 2 + 1]
        pair_do = jnp.concatenate([low, high], axis=1)
        both = jnp.concatenate([ds_r[pair * 2], ds_r[pair * 2 + 1]], axis=1)
        dq = jnp.zeros((T, 2 * T), F32)
        for tile in range(4):
            rows = slice(tile * 256, (tile + 1) * 256)
            probs = jnp.exp2(masked(tile, pair_q, spots) - both[0:1, :])
            dprobs = nn(v_all[2 * tile : 2 * tile + 2].reshape(2 * T, T), pair_do)
            dscores = (probs * (dprobs - both[1:2, :])).astype(BF16)
            dv_acc[rows, :] += nt(probs.astype(BF16), pair_do)
            dk_acc[rows, :] += nn(dscores, pair_q)
            dq = dq + nn(kt[:, rows], dscores)
        for e in (0, 1):
            dq_s[pair * 2 + e] = (dq[:, e * T : (e + 1) * T] * scale).astype(BF16)
        return 0

    lax.fori_loop(0, 4, grad, 0)
    dkv_s[:, 0:T, :] = (dk_acc[...] * scale).astype(BF16).reshape(N, T, T)
    dkv_s[:, T : 2 * T, :] = dv_acc[...].astype(BF16).reshape(N, T, T)
    dkv_here = spread(c_peer, lambda p: dkv_s.at[p], dkv_r, c)
    dkv_r[c] = dkv_s[c]
    dq_here = spread(y_peer, lambda p: dq_s.at[p], dq_r, y)
    dq_r[y] = dq_s[y]

    cg1_here()
    for lo in (0, 16):
        cg2_s[:, lo : lo + 16, :] = (
            nn(order_out, cg1[:, lo : lo + 16, :].reshape(T, T)).astype(BF16).reshape(N, 16, T)
        )
    cg2[y] = cg2_s[y]
    cg2_here = spread(y_peer, lambda p: cg2_s.at[p], cg2, y)

    dq_here()
    grad_q = dq_r[0].astype(F32)
    for i in range(1, N):
        grad_q = grad_q + dq_r[i].astype(F32)
    packed[0] = grad_q.T.astype(BF16)
    dkv_here()
    grad_kv = dkv_r[0].astype(F32)
    for i in range(1, N):
        grad_kv = grad_kv + dkv_r[i].astype(F32)
    packed[1] = grad_kv[0:T].astype(BF16)
    packed[2] = grad_kv[T : 2 * T].astype(BF16)

    cg2_here()
    packed[3] = flip(up_t[...] * cg2[:, 0:16, :].reshape(T, T).astype(F32)).astype(BF16)
    packed[5] = flip(cg2[:, 16:32, :].reshape(T, T)).astype(BF16)

    for sem, dst in enumerate(started):
        part = dst.at[pl.ds(0, N - 1)]
        pltpu.make_async_copy(part, part, send.at[sem]).wait()


def unpack(packed, *rest):
    outs, done = rest[:-1], rest[-1]
    moves = [pltpu.make_async_copy(packed.at[i], out, done.at[i]) for i, out in enumerate(outs)]
    for move in moves:
        move.start()
    for move in moves:
        move.wait()


def per_device(queries, keys_in, values, hq, hv, taps, gain, upstream, order):
    def vmem(*shape, dtype=BF16):
        return pltpu.VMEM(shape, dtype)

    pair16 = vmem(N, 16, T)
    pair32 = vmem(N, 32, T)
    square = vmem(N, T, T)
    tall = vmem(N, 2 * T, T)
    lines = vmem(N, 2, T, dtype=F32)
    wide = vmem(T, T, dtype=F32)
    one = vmem(T, T)
    in_hbm = pl.BlockSpec(memory_space=pltpu.HBM)
    packed = pl.pallas_call(
        kernel,
        out_shape=jax.ShapeDtypeStruct((6, T, T), BF16),
        in_specs=[in_hbm] * 9,
        out_specs=pl.BlockSpec(memory_space=pltpu.VMEM),
        scratch_shapes=[
            pltpu.SMEM((1, T), jnp.int32), vmem(1, T, dtype=jnp.int32), one, one, one, vmem(1, T, dtype=F32), one,
            square, square, square, vmem(T, N * T), vmem(T, N * T), vmem(N * T, 2 * T, dtype=F32),
            pair32, pair32, pair32, pair32, square, square, lines, lines, pair16, pair16, pair16, pair16,
            vmem(1, T, dtype=F32), vmem(N, 1, T, dtype=F32), vmem(1, T, dtype=F32), vmem(N, 1, T, dtype=F32),
            one, square, vmem(2, T, dtype=F32), lines, pair16, pair16, pair16, pair16,
            pair32, pair32, pair32, pair32, square, square, tall, tall,
            wide, wide, wide, wide, vmem(2, T, SEQ), vmem(2, HALF, T, dtype=F32), vmem(2, 2 * T, T, dtype=F32),
            vmem(N * T, T, dtype=F32), vmem(N * T, T, dtype=F32),
            pltpu.SemaphoreType.DMA((20,)), pltpu.SemaphoreType.DMA((20,)), pltpu.SemaphoreType.DMA((10,)),
        ],
        compiler_params=pltpu.CompilerParams(
            collective_id=0, has_side_effects=True, vmem_limit_bytes=60 * 1024 * 1024
        ),
        name="pair_backward",
    )(order.reshape(1, -1), queries, keys_in, values, hq, hv, taps, gain.reshape(1, -1), upstream)
    return pl.pallas_call(
        unpack,
        out_shape=(jax.ShapeDtypeStruct((T, T), BF16),) * 6,
        in_specs=[in_hbm],
        out_specs=(in_hbm,) * 6,
        scratch_shapes=[pltpu.SemaphoreType.DMA((6,))],
        compiler_params=pltpu.CompilerParams(vmem_limit_bytes=60 * 1024 * 1024),
        name="unpack",
    )(packed)


def solution(mesh):
    rows = P("ctx", "ch")
    return jax.shard_map(
        per_device,
        mesh=mesh,
        in_specs=(rows,) * 6 + (P("ch"), rows, P()),
        out_specs=(rows,) * 6,
        check_vma=False,
    )
```

time: 104 us -> 90.6 us (0.87)
  the two profiles are of different devices: /device:TPU:1 before, /device:TPU:8 now
where the time goes in v2:
time: 90.6 us; the launch traced here: 90.4 us
  Pallas kernels  89.7 us (99%)
    pallas_call x1, Pallas kernels, per_device(): pl.pallas_call(kernel, out_shape=jax.ShapeDtypeStruct((6, T, T), BF16), i...  82.6 us
    pallas_call x1, Pallas kernels, per_device(): pl.pallas_call(unpack, out_shape=(jax.ShapeDtypeStruct((T, T), BF16),) *...  7.11 us

profile of v2, /device:TPU:8, one launch (start us, length us, event | category | flops | bytes accessed | tf_op | source)
XLA Modules:
  0.0 90.4 jit_solution(6729474963683561632)
XLA Ops:
  0.6 82.6 %pair_backward.1.packed = bf16[6,128,128]{2,1,0:T(8,128)(2,1)} custom-call(s32[1,128]{1,0:T(1,128)} %bitcast.2, bf16[128,128]{1,0:T(8,128)(2,1)} %q_h.1, bf16[128,128]{1,0:T(8,128)(2,1)} %k_h.1, bf16[128,128]{1,0:T(8,128)(2,1)} %v_h.1, bf16[128,128]{1,0:T(8,128)(2,1)} %hq_h.1, bf16[128,128]{1,0:T(8,128)(2,1)} %hv_h.1, bf16[128,128]{1,0:T(8,128)(2,1)} %taps_h.1, ...), custom_call_target="tpu_custom_call" | custom-call | tf_op jit(solution)/shard_map/pair_backward/pallas_call | solution.py:483
  83.3 7.1 %unpack.1 = (bf16[128,128]{1,0:T(8,128)(2,1)}, bf16[128,128]{1,0:T(8,128)(2,1)}, bf16[128,128]{1,0:T(8,128)(2,1)}, bf16[128,128]{1,0:T(8,128)(2,1)}, bf16[128,128]{1,0:T(8,128)(2,1)}, /*index=5*/bf16[128,128]{1,0:T(8,128)(2,1)}) custom-call(bf16[6,128,128]{2,1,0:T(8,128)(2,1)} %pair_backward.1.packed), custom_call_target="tpu_custom_call" | custom-call | tf_op jit(solution)/shard_map/unpack/pallas_call | solution.py:504

commit v3 on v2

--- a/solution.py
+++ b/solution.py
@@ -40,21 +40,23 @@
 
 
 def row_source(r):
-    return (r & 7) * N + (r >> 4)
+    return r >> 1
 
 
 def row_channel(r):
-    return (r >> 3) & 1
-
-
-def to_rows():
-    out, inn = iota((T, T), 0), iota((T, T), 1)
-    return one_hot(inn == (out & 7) * 16 + (out >> 4) * 2 + ((out >> 3) & 1))
-
-
-def from_rows():
-    inn, out = iota((T, T), 1), iota((T, T), 0)
-    return one_hot(out == (inn & 7) * 16 + (inn >> 4) * 2 + ((inn >> 3) & 1))
+    return r & 1
+
+
+def interleave(first, second):
+    out, inn = iota((2 * T, T), 0), iota((2 * T, T), 1)
+    return sum(
+        nn(one_hot(out == (inn >> 1) * 4 + 2 * k + (inn & 1)), field) for k, field in enumerate((first, second))
+    ).astype(BF16)
+
+
+def separate(rows, k):
+    out, inn = iota((T, 2 * T), 0), iota((T, 2 * T), 1)
+    return nn(one_hot(inn == (out >> 1) * 4 + 2 * k + (out & 1)), rows).astype(BF16)
 
 
 def toeplitz(chunks, table, first):
@@ -104,10 +106,9 @@
     packed,
     order_s, order_v, hq_ref, hv_ref, taps_ref, gain_ref, up_ref,
     q_all, k_all, v_all, vt, kt, scores,
-    tg1_s, tg1, tg2_s, tg2, o_s, o_r, os_s, os_r, bm1_s, bm1, bm2_s, bm2,
-    ss_s, ss_r, in_s, in_r, do_s, do_r, ds_s, ds_r, mx1_s, mx1, mx2_s, mx2,
-    cg1_s, cg1, cg2_s, cg2, dq_s, dq_r, dkv_s, dkv_r,
-    up_t, hv_t, hvg_t, gain_t, table, chunks, steps, dk_acc, dv_acc,
+    tg_s, tg, o_s, o_r, os_s, os_r, bm_s, bm, st_s, st_r, sc_s, sc_all, at_s, at_all, ds_s, ds_r, do_all,
+    mx_s, mx, cg_s, cg, dq_s, dq_r, dkv_s, dkv_r,
+    up_t, hv_t, hvg_t, gain_t, table, chunks, steps, dq_acc,
     send, recv, load,
 ):
     me = lax.axis_index("ctx")
@@ -129,40 +130,55 @@
         p = lax.rem(head + k, N)
         return p, (me, p)
 
+    def all_peer(k):
+        p = lax.rem(me + k, N * N)
+        return p, (p, head)
+
     started = []
 
-    def spread(peer, src, dst, slot):
+    def channel(dst):
         sem = len(started)
         started.append(dst)
-
-        def step(k, _):
-            p, device = peer(k)
+        others = dst.shape[0] - 1
+
+        def post(src, slot, device):
             pltpu.make_async_remote_copy(
-                src_ref=src(p),
+                src_ref=src,
                 dst_ref=dst.at[slot],
                 send_sem=send.at[sem],
                 recv_sem=recv.at[sem],
                 device_id=device,
                 device_id_type=MESH,
             ).start()
+
+        def arrived():
+            part = dst.at[pl.ds(0, others)]
+            pltpu.make_async_copy(part, part, recv.at[sem]).wait()
+
+        return post, arrived
+
+    def spread(peer, src, dst, slot):
+        post, arrived = channel(dst)
+
+        def step(k, _):
+            p, device = peer(k)
+            post(src(p), slot, device)
             return 0
 
-        lax.fori_loop(1, N, step, 0)
-
-        def arrived():
-            part = dst.at[pl.ds(0, N - 1)]
-            pltpu.make_async_copy(part, part, recv.at[sem]).wait()
-
+        lax.fori_loop(1, dst.shape[0], step, 0)
         return arrived
 
     barrier = pltpu.get_barrier_semaphore()
 
-    def greet(k, _):
-        for peer in (y_peer, c_peer, h_peer):
+    def greet(peer):
+        def step(k, _):
             pl.semaphore_signal(barrier, inc=1, device_id=peer(k)[1], device_id_type=MESH)
-        return 0
-
-    lax.fori_loop(1, N, greet, 0)
+            return 0
+
+        return step
+
+    lax.fori_loop(1, N * N, greet(all_peer), 0)
+    lax.fori_loop(1, N, greet(h_peer), 0)
 
     loads = [
         pltpu.make_async_copy(src, dst, load.at[i])
@@ -179,14 +195,13 @@
         each.wait()
     up = up_ref[...].astype(F32)
     gated = (up * hq_ref[...].astype(F32)).astype(BF16)
-    tg1_s[:, 0:16, :] = flip(gated).astype(BF16).reshape(N, 16, T)
-    tg1_s[:, 16:32, :] = flip(taps_ref[...]).astype(BF16).reshape(N, 16, T)
-    tg1[y] = tg1_s[y]
+    tg_s[...] = interleave(flip(gated).astype(BF16), flip(taps_ref[...]).astype(BF16)).reshape(N * N, 4, T)
+    tg[me] = tg_s[me]
     for each in loads[3:]:
         each.wait()
-    pl.semaphore_wait(barrier, 3 * (N - 1))
-
-    tg1_here = spread(y_peer, lambda p: tg1_s.at[p], tg1, y)
+    pl.semaphore_wait(barrier, N * N - 1 + N - 1)
+
+    tg_here = spread(all_peer, lambda p: tg_s.at[p], tg, me)
     k_here = spread(c_peer, lambda p: k_all.at[c], k_all, c)
     q_here = spread(y_peer, lambda p: q_all.at[y], q_all, y)
     v_here = spread(c_peer, lambda p: v_all.at[c], v_all, c)
@@ -196,8 +211,7 @@
     gain_t[...] = jnp.broadcast_to(gain_ref[...], (T, T)).T
     hvg_t[...] = hv_t[...] * gain_t[...]
     steps[:, 0:T, :] = jnp.zeros((2, T, T), F32)
-    dk_acc[...] = jnp.zeros((N * T, T), F32)
-    dv_acc[...] = jnp.zeros((N * T, T), F32)
+    dq_acc[...] = jnp.zeros((T, N * T), F32)
 
     lane = iota((T, T), 1)
     line = iota((T, T), 0)
@@ -248,7 +262,7 @@
         return spot + base
 
     def masked(tile, pair_q, spots):
-        keys = k_all[2 * tile : 2 * tile + 2].reshape(2 * T, T)
+        keys = k_all[pl.ds(2 * tile, 2)].reshape(2 * T, T)
         raw = nt(keys, pair_q) * (scale * LOG2E)
         out = []
         for e in range(4):
@@ -258,7 +272,8 @@
             )
         return jnp.concatenate(out, axis=0)
 
-    def attend(pair, _):
+    def attend(turn, _):
+        pair = lax.rem(turn + lax.div(y, 2), 4)
         pair_q = q_all[pl.ds(pair * 2, 2)].reshape(2 * T, T)
         spots = query_places(pair)
         peak = jnp.full((1, 2 * T), HIDDEN, F32)
@@ -273,40 +288,22 @@
             total = total + jnp.sum(weights, axis=0, keepdims=True)
             out = out + nn(vt[:, tile * 256 : (tile + 1) * 256], weights.astype(BF16))
         for e in (0, 1):
+            p = pair * 2 + e
             lanes = slice(e * T, (e + 1) * T)
-            o_s[pair * 2 + e] = out[:, lanes].astype(BF16)
-            os_s[pair * 2 + e] = jnp.concatenate([peak[:, lanes], total[:, lanes]], axis=0)
+            o_s[p] = out[:, lanes].astype(BF16)
+            os_s[p] = jnp.concatenate([peak[:, lanes], total[:, lanes]], axis=0)
+
+            @pl.when(p != y)
+            def _():
+                os_post(os_s.at[p], y, (p * N + c, head))
+                o_post(o_s.at[p], y, (p * N + c, head))
+
         return 0
 
-    def forward_part():
-        k_here()
-        q_here()
-        v_here()
-        for i in range(N):
-            vt[:, i * T : (i + 1) * T] = flip(v_all[i]).astype(BF16)
-            kt[:, i * T : (i + 1) * T] = flip(k_all[i]).astype(BF16)
-        lax.fori_loop(0, 4, attend, 0)
-        o_r[y] = o_s[y]
-        os_r[y] = os_s[y]
-        os_here = spread(y_peer, lambda p: os_s.at[p], os_r, y)
-        o_here = spread(y_peer, lambda p: o_s.at[p], o_r, y)
-        return os_here, o_here
-
-    tg1_here()
-    order_in = to_rows()
-    order_out = from_rows()
-    for lo in (0, 16):
-        tg2_s[:, lo : lo + 16, :] = (
-            nn(order_in, tg1[:, lo : lo + 16, :].reshape(T, T)).astype(BF16).reshape(N, 16, T)
-        )
-    tg2[c] = tg2_s[c]
-    tg2_here = spread(c_peer, lambda p: tg2_s.at[p], tg2, c)
-
-    os_here, o_here = forward_part()
-
-    tg2_here()
-    grads = tg2[:, 0:16, :].reshape(T, T)
-    taps = tg2[:, 16:32, :].reshape(T, T)
+    tg_here()
+    both_rows = tg[...].reshape(2 * T, T)
+    grads = separate(both_rows, 0)
+    taps = separate(both_rows, 1)
     narrow_lane, narrow_line = iota((HALF, T), 1), iota((HALF, T), 0)
     narrow_ours = [row_channel(narrow_lane) == j for j in (0, 1)]
     for j in (0, 1):
@@ -315,9 +312,21 @@
     lay_out(grads, False, True)
     backs = [(r * tap_scale).astype(BF16) for r in long_products(table, steps, HALF)]
     flipped_t = [T - 1 - p for p in place_t]
-    bm1_s[...] = collect(backs, flipped_t, 0, False).reshape(N, 16, T)
-    bm1[c] = bm1_s[c]
-    bm1_here = spread(c_peer, lambda p: bm1_s.at[p], bm1, c)
+    bm_s[...] = collect(backs, flipped_t, 0, False).reshape(N * N, 2, T)
+    bm[me] = bm_s[me]
+    bm_here = spread(all_peer, lambda p: bm_s.at[p], bm, me)
+
+    k_here()
+    q_here()
+    v_here()
+    for i in range(N):
+        vt[:, i * T : (i + 1) * T] = flip(v_all[i]).astype(BF16)
+        kt[:, i * T : (i + 1) * T] = flip(k_all[i]).astype(BF16)
+    os_post, os_here = channel(os_r)
+    o_post, o_here = channel(o_r)
+    lax.fori_loop(0, 4, attend, 0)
+    o_r[y] = o_s[y]
+    os_r[y] = os_s[y]
 
     flats = [jnp.zeros((HALF, T), F32)] * 2
     for h in (0, 1):
@@ -330,6 +339,13 @@
     for j in (0, 1):
         chunks[j] = flats[j]
     toeplitz(chunks, table, HALF)
+
+    bm_here()
+    back = bm[...].reshape(T, T).astype(F32)
+    sc_s[...] = (back * hvg_t[...]).astype(BF16)
+    sc_all[y] = sc_s[...]
+    sc_here = spread(y_peer, lambda p: sc_s, sc_all, y)
+    scaled = sc_s[...].astype(F32)
 
     os_here()
     o_here()
@@ -343,100 +359,88 @@
         total = total + factor * os_r[i, 1:2, :]
         mix = mix + factor * o_r[i].astype(F32)
     lse = peak + jnp.log2(total)
-    act = (mix / total).astype(BF16).astype(F32)
-    ss_s[...] = jnp.sum(act * act, axis=0, keepdims=True)
-    ss_r[head] = ss_s[...]
-    ss_here = spread(h_peer, lambda p: ss_s, ss_r, head)
-
-    bm1_here()
-    bm2_s[...] = nn(order_out, bm1[...].reshape(T, T)).astype(BF16).reshape(N, 16, T)
-    bm2[y] = bm2_s[y]
-    bm2_here = spread(y_peer, lambda p: bm2_s.at[p], bm2, y)
-
-    ss_here()
-    square = ss_r[0]
+    at_s[...] = (mix / total).astype(BF16)
+    act = at_s[...].astype(F32)
+    st_s[...] = jnp.concatenate(
+        [jnp.sum(act * act, axis=0, keepdims=True), jnp.sum(scaled * act, axis=0, keepdims=True)],
+        axis=0,
+    )
+    st_r[head] = st_s[...]
+    st_here = spread(h_peer, lambda p: st_s, st_r, head)
+    at_all[y] = at_s[...]
+    at_here = spread(y_peer, lambda p: at_s, at_all, y)
+
+    st_here()
+    sums = st_r[0]
     for i in range(1, N):
-        square = square + ss_r[i]
-    inv_root = lax.rsqrt(square / WIDTH + 1e-06)
-    normed = act * inv_root * gain_t[...]
-    mx1_s[...] = (normed * hv_t[...]).astype(BF16).reshape(N, 16, T)
-    mx1[y] = mx1_s[y]
-    mx1_here = spread(y_peer, lambda p: mx1_s.at[p], mx1, y)
-
-    bm2_here()
-    back = bm2[...].reshape(T, T).astype(F32)
-    scaled = back * hvg_t[...]
-    in_s[...] = jnp.sum(scaled * act, axis=0, keepdims=True)
-    in_r[head] = in_s[...]
-    in_here = spread(h_peer, lambda p: in_s, in_r, head)
-    packed[4] = flip((back * normed).astype(BF16)).astype(BF16)
-
-    mx1_here()
-    mx2_s[...] = nn(order_in, mx1[...].reshape(T, T)).astype(BF16).reshape(N, 16, T)
-    mx2[c] = mx2_s[c]
-    mx2_here = spread(c_peer, lambda p: mx2_s.at[p], mx2, c)
-
-    in_here()
-    inner = in_r[0]
-    for i in range(1, N):
-        inner = inner + in_r[i]
-    grad_att = (
-        inv_root * scaled - act * (inv_root * inv_root * inv_root) * (inner / WIDTH)
-    ).astype(BF16)
-    do_s[...] = grad_att
-    do_r[y] = grad_att
-    do_here = spread(y_peer, lambda p: do_s, do_r, y)
+        sums = sums + st_r[i]
+    inv_root = lax.rsqrt(sums[0:1, :] / WIDTH + 1e-06)
+    pull = (inv_root * inv_root * inv_root) * (sums[1:2, :] / WIDTH)
+    grad_att = (inv_root * scaled - act * pull).astype(BF16)
     delta = jnp.sum(grad_att.astype(F32) * act, axis=0, keepdims=True)
-    ds_s[...] = jnp.concatenate([lse, delta], axis=0)
+    ds_s[...] = jnp.concatenate([lse, delta, inv_root, pull], axis=0)
     ds_r[y] = ds_s[...]
     ds_here = spread(y_peer, lambda p: ds_s, ds_r, y)
-
-    mx2_here()
-    lay_out(mx2[...].reshape(T, T), True, False)
+    normed = act * inv_root * gain_t[...]
+    mx_s[...] = (normed * hv_t[...]).astype(BF16).reshape(N * N, 2, T)
+    mx[me] = mx_s[me]
+    mx_here = spread(all_peer, lambda p: mx_s.at[p], mx, me)
+    packed[4] = flip((back * normed).astype(BF16)).astype(BF16)
+
+    sc_here()
+    at_here()
+    ds_here()
+    for i in range(N):
+        do_all[i] = (
+            ds_r[i, 2:3, :] * sc_all[i].astype(F32) - at_all[i].astype(F32) * ds_r[i, 3:4, :]
+        ).astype(BF16)
+    dkv_post, dkv_here = channel(dkv_r)
+
+    def grad(turn, _):
+        tile = lax.rem(turn + lax.div(c, 2), 4)
+        rows = pl.ds(pl.multiple_of(tile * 2 * T, 2 * T), 2 * T)
+        tile_v = v_all[pl.ds(2 * tile, 2)].reshape(2 * T, T)
+        dk = jnp.zeros((2 * T, T), F32)
+        dv = jnp.zeros((2 * T, T), F32)
+        for pair in range(4):
+            pair_q = q_all[pair * 2 : pair * 2 + 2].reshape(2 * T, T)
+            pair_do = jnp.concatenate([do_all[pair * 2], do_all[pair * 2 + 1]], axis=1)
+            both = jnp.concatenate([ds_r[pair * 2], ds_r[pair * 2 + 1]], axis=1)
+            probs = jnp.exp2(masked(tile, pair_q, query_places(pair)) - both[0:1, :])
+            dprobs = nn(tile_v, pair_do)
+            dscores = (probs * (dprobs - both[1:2, :])).astype(BF16)
+            dv = dv + nt(probs.astype(BF16), pair_do)
+            dk = dk + nn(dscores, pair_q)
+            dq_acc[:, pair * 2 * T : (pair + 1) * 2 * T] += nn(kt[:, rows], dscores)
+        dk = (dk * scale).astype(BF16)
+        dv = dv.astype(BF16)
+        for e in (0, 1):
+            p = tile * 2 + e
+            dkv_s[p, 0:T, :] = dk[e * T : (e + 1) * T]
+            dkv_s[p, T : 2 * T, :] = dv[e * T : (e + 1) * T]
+
+            @pl.when(p != c)
+            def _():
+                dkv_post(dkv_s.at[p], c, (y * N + p, head))
+
+        return 0
+
+    lax.fori_loop(0, 4, grad, 0)
+    for i in range(N):
+        dq_s[i] = (dq_acc[:, i * T : (i + 1) * T] * scale).astype(BF16)
+    dq_here = spread(y_peer, lambda p: dq_s.at[p], dq_r, y)
+    dq_r[y] = dq_s[y]
+    dkv_r[c] = dkv_s[c]
+
+    mx_here()
+    lay_out(mx[...].reshape(T, T), True, False)
     lates = [(r * tap_scale).astype(BF16) for r in long_products(table, steps, T)]
     lag_t = [T - 1 - (row_source(line) * 2 + h) for h in (0, 1)]
-    cg1_s[:, 0:16, :] = collect(lates, place_t, 0, True).reshape(N, 16, T)
-    cg1_s[:, 16:32, :] = collect(lates, lag_t, HALF, False).reshape(N, 16, T)
-    cg1[c] = cg1_s[c]
-    cg1_here = spread(c_peer, lambda p: cg1_s.at[p], cg1, c)
-
-    do_here()
-    ds_here()
-
-    def grad(pair, _):
-        pair_q = q_all[pl.ds(pair * 2, 2)].reshape(2 * T, T)
-        spots = query_places(pair)
-        low, high = do_r[pair * 2], do_r[pair * 2 + 1]
-        pair_do = jnp.concatenate([low, high], axis=1)
-        both = jnp.concatenate([ds_r[pair * 2], ds_r[pair * 2 + 1]], axis=1)
-        dq = jnp.zeros((T, 2 * T), F32)
-        for tile in range(4):
-            rows = slice(tile * 256, (tile + 1) * 256)
-            probs = jnp.exp2(masked(tile, pair_q, spots) - both[0:1, :])
-            dprobs = nn(v_all[2 * tile : 2 * tile + 2].reshape(2 * T, T), pair_do)
-            dscores = (probs * (dprobs - both[1:2, :])).astype(BF16)
-            dv_acc[rows, :] += nt(probs.astype(BF16), pair_do)
-            dk_acc[rows, :] += nn(dscores, pair_q)
-            dq = dq + nn(kt[:, rows], dscores)
-        for e in (0, 1):
-            dq_s[pair * 2 + e] = (dq[:, e * T : (e + 1) * T] * scale).astype(BF16)
-        return 0
-
-    lax.fori_loop(0, 4, grad, 0)
-    dkv_s[:, 0:T, :] = (dk_acc[...] * scale).astype(BF16).reshape(N, T, T)
-    dkv_s[:, T : 2 * T, :] = dv_acc[...].astype(BF16).reshape(N, T, T)
-    dkv_here = spread(c_peer, lambda p: dkv_s.at[p], dkv_r, c)
-    dkv_r[c] = dkv_s[c]
-    dq_here = spread(y_peer, lambda p: dq_s.at[p], dq_r, y)
-    dq_r[y] = dq_s[y]
-
-    cg1_here()
-    for lo in (0, 16):
-        cg2_s[:, lo : lo + 16, :] = (
-            nn(order_out, cg1[:, lo : lo + 16, :].reshape(T, T)).astype(BF16).reshape(N, 16, T)
-        )
-    cg2[y] = cg2_s[y]
-    cg2_here = spread(y_peer, lambda p: cg2_s.at[p], cg2, y)
+    cg_s[...] = interleave(
+        collect(lates, place_t, 0, True), collect(lates, lag_t, HALF, False)
+    ).reshape(N * N, 4, T)
+    cg[me] = cg_s[me]
+    cg_here = spread(all_peer, lambda p: cg_s.at[p], cg, me)
 
     dq_here()
     grad_q = dq_r[0].astype(F32)
@@ -450,12 +454,13 @@
     packed[1] = grad_kv[0:T].astype(BF16)
     packed[2] = grad_kv[T : 2 * T].astype(BF16)
 
-    cg2_here()
-    packed[3] = flip(up_t[...] * cg2[:, 0:16, :].reshape(T, T).astype(F32)).astype(BF16)
-    packed[5] = flip(cg2[:, 16:32, :].reshape(T, T)).astype(BF16)
+    cg_here()
+    results = cg[...].reshape(2 * T, T)
+    packed[3] = flip(up_t[...] * separate(results, 0).astype(F32)).astype(BF16)
+    packed[5] = flip(separate(results, 1)).astype(BF16)
 
     for sem, dst in enumerate(started):
-        part = dst.at[pl.ds(0, N - 1)]
+        part = dst.at[pl.ds(0, dst.shape[0] - 1)]
         pltpu.make_async_copy(part, part, send.at[sem]).wait()
 
 
@@ -472,8 +477,8 @@
     def vmem(*shape, dtype=BF16):
         return pltpu.VMEM(shape, dtype)
 
-    pair16 = vmem(N, 16, T)
-    pair32 = vmem(N, 32, T)
+    twos = vmem(N * N, 2, T)
+    fours = vmem(N * N, 4, T)
     square = vmem(N, T, T)
     tall = vmem(N, 2 * T, T)
     lines = vmem(N, 2, T, dtype=F32)
@@ -488,13 +493,12 @@
         scratch_shapes=[
             pltpu.SMEM((1, T), jnp.int32), vmem(1, T, dtype=jnp.int32), one, one, one, vmem(1, T, dtype=F32), one,
             square, square, square, vmem(T, N * T), vmem(T, N * T), vmem(N * T, 2 * T, dtype=F32),
-            pair32, pair32, pair32, pair32, square, square, lines, lines, pair16, pair16, pair16, pair16,
-            vmem(1, T, dtype=F32), vmem(N, 1, T, dtype=F32), vmem(1, T, dtype=F32), vmem(N, 1, T, dtype=F32),
-            one, square, vmem(2, T, dtype=F32), lines, pair16, pair16, pair16, pair16,
-            pair32, pair32, pair32, pair32, square, square, tall, tall,
+            fours, fours, square, square, lines, lines, twos, twos, vmem(2, T, dtype=F32), lines,
+            one, square, one, square, vmem(4, T, dtype=F32), vmem(N, 4, T, dtype=F32), square,
+            twos, twos, fours, fours, square, square, tall, tall,
             wide, wide, wide, wide, vmem(2, T, SEQ), vmem(2, HALF, T, dtype=F32), vmem(2, 2 * T, T, dtype=F32),
-            vmem(N * T, T, dtype=F32), vmem(N * T, T, dtype=F32),
-            pltpu.SemaphoreType.DMA((20,)), pltpu.SemaphoreType.DMA((20,)), pltpu.SemaphoreType.DMA((10,)),
+            vmem(T, N * T, dtype=F32),
+            pltpu.SemaphoreType.DMA((15,)), pltpu.SemaphoreType.DMA((15,)), pltpu.SemaphoreType.DMA((10,)),
         ],
         compiler_params=pltpu.CompilerParams(
             collective_id=0, has_side_effects=True, vmem_limit_bytes=60 * 1024 * 1024

time: 90.6 us -> 84.6 us (0.934)
  the two profiles are of different devices: /device:TPU:8 before, /device:TPU:1 now
where the time goes in v3:
time: 84.6 us; the launch traced here: 84.4 us
  Pallas kernels  83.7 us (99%)
    pallas_call x1, Pallas kernels, per_device(): pl.pallas_call(kernel, out_shape=jax.ShapeDtypeStruct((6, T, T), BF16), i...  76.6 us
    pallas_call x1, Pallas kernels, per_device(): pl.pallas_call(unpack, out_shape=(jax.ShapeDtypeStruct((T, T), BF16),) *...  7.11 us

profile of v3, /device:TPU:1, one launch (start us, length us, event | category | flops | bytes accessed | tf_op | source)
XLA Modules:
  0.0 84.4 jit_solution(14583737464977311770)
XLA Ops:
  0.6 76.6 %pair_backward.1.packed = bf16[6,128,128]{2,1,0:T(8,128)(2,1)} custom-call(s32[1,128]{1,0:T(1,128)} %bitcast.2, bf16[128,128]{1,0:T(8,128)(2,1)} %q_h.1, bf16[128,128]{1,0:T(8,128)(2,1)} %k_h.1, bf16[128,128]{1,0:T(8,128)(2,1)} %v_h.1, bf16[128,128]{1,0:T(8,128)(2,1)} %hq_h.1, bf16[128,128]{1,0:T(8,128)(2,1)} %hv_h.1, bf16[128,128]{1,0:T(8,128)(2,1)} %taps_h.1, ...), custom_call_target="tpu_custom_call" | custom-call | tf_op jit(solution)/shard_map/pair_backward/pallas_call | solution.py:488
  77.3 7.1 %unpack.1 = (bf16[128,128]{1,0:T(8,128)(2,1)}, bf16[128,128]{1,0:T(8,128)(2,1)}, bf16[128,128]{1,0:T(8,128)(2,1)}, bf16[128,128]{1,0:T(8,128)(2,1)}, bf16[128,128]{1,0:T(8,128)(2,1)}, /*index=5*/bf16[128,128]{1,0:T(8,128)(2,1)}) custom-call(bf16[6,128,128]{2,1,0:T(8,128)(2,1)} %pair_backward.1.packed), custom_call_target="tpu_custom_call" | custom-call | tf_op jit(solution)/shard_map/unpack/pallas_call | solution.py:508

commit v4 on v3

--- a/solution.py
+++ b/solution.py
@@ -109,7 +109,7 @@
     tg_s, tg, o_s, o_r, os_s, os_r, bm_s, bm, st_s, st_r, sc_s, sc_all, at_s, at_all, ds_s, ds_r, do_all,
     mx_s, mx, cg_s, cg, dq_s, dq_r, dkv_s, dkv_r,
     up_t, hv_t, hvg_t, gain_t, table, chunks, steps, dq_acc,
-    send, recv, load,
+    send, recv, load, grid_sem,
 ):
     me = lax.axis_index("ctx")
     head = lax.axis_index("ch")
@@ -170,15 +170,15 @@
 
     barrier = pltpu.get_barrier_semaphore()
 
-    def greet(peer):
+    def greet(sem, peer):
         def step(k, _):
-            pl.semaphore_signal(barrier, inc=1, device_id=peer(k)[1], device_id_type=MESH)
+            pl.semaphore_signal(sem, inc=1, device_id=peer(k)[1], device_id_type=MESH)
             return 0
 
         return step
 
-    lax.fori_loop(1, N * N, greet(all_peer), 0)
-    lax.fori_loop(1, N, greet(h_peer), 0)
+    for peer in (c_peer, y_peer, h_peer):
+        lax.fori_loop(1, N, greet(barrier, peer), 0)
 
     loads = [
         pltpu.make_async_copy(src, dst, load.at[i])
@@ -199,8 +199,10 @@
     tg[me] = tg_s[me]
     for each in loads[3:]:
         each.wait()
-    pl.semaphore_wait(barrier, N * N - 1 + N - 1)
-
+    pl.semaphore_wait(barrier, 3 * (N - 1))
+    lax.fori_loop(1, N, greet(grid_sem, y_peer), 0)
+
+    pl.semaphore_wait(grid_sem, N - 1)
     tg_here = spread(all_peer, lambda p: tg_s.at[p], tg, me)
     k_here = spread(c_peer, lambda p: k_all.at[c], k_all, c)
     q_here = spread(y_peer, lambda p: q_all.at[y], q_all, y)
@@ -464,13 +466,9 @@
         pltpu.make_async_copy(part, part, send.at[sem]).wait()
 
 
-def unpack(packed, *rest):
-    outs, done = rest[:-1], rest[-1]
-    moves = [pltpu.make_async_copy(packed.at[i], out, done.at[i]) for i, out in enumerate(outs)]
-    for move in moves:
-        move.start()
-    for move in moves:
-        move.wait()
+def unpack(packed, *outs):
+    for i, out in enumerate(outs):
+        out[...] = packed[i]
 
 
 def per_device(queries, keys_in, values, hq, hv, taps, gain, upstream, order):
@@ -499,6 +497,7 @@
             wide, wide, wide, wide, vmem(2, T, SEQ), vmem(2, HALF, T, dtype=F32), vmem(2, 2 * T, T, dtype=F32),
             vmem(T, N * T, dtype=F32),
             pltpu.SemaphoreType.DMA((15,)), pltpu.SemaphoreType.DMA((15,)), pltpu.SemaphoreType.DMA((10,)),
+            pltpu.SemaphoreType.REGULAR,
         ],
         compiler_params=pltpu.CompilerParams(
             collective_id=0, has_side_effects=True, vmem_limit_bytes=60 * 1024 * 1024
@@ -508,10 +507,8 @@
     return pl.pallas_call(
         unpack,
         out_shape=(jax.ShapeDtypeStruct((T, T), BF16),) * 6,
-        in_specs=[in_hbm],
-        out_specs=(in_hbm,) * 6,
-        scratch_shapes=[pltpu.SemaphoreType.DMA((6,))],
-        compiler_params=pltpu.CompilerParams(vmem_limit_bytes=60 * 1024 * 1024),
+        in_specs=[pl.BlockSpec(memory_space=pltpu.VMEM)],
+        out_specs=(pl.BlockSpec(memory_space=pltpu.VMEM),) * 6,
         name="unpack",
     )(packed)
 

time: 84.6 us -> 78.6 us (0.929)
  Pallas kernels: 83.7 us -> 77.7 us
    pallas_call x1, Pallas kernels: 7.11 us -> 1.6 us  [per_device(): pl.pallas_call(unpack, out_shape=(jax.ShapeDtypeStruct((T, T), BF16),) *...]
where the time goes in v4:
time: 78.6 us; the launch traced here: 78.4 us
  Pallas kernels  77.7 us (99%)
    pallas_call x1, Pallas kernels, per_device(): pl.pallas_call(kernel, out_shape=jax.ShapeDtypeStruct((6, T, T), BF16), i...  76.1 us
    pallas_call x1, Pallas kernels, per_device(): pl.pallas_call(unpack, out_shape=(jax.ShapeDtypeStruct((T, T), BF16),) *...  1.6 us

profile of v4, /device:TPU:1, one launch (start us, length us, event | category | flops | bytes accessed | tf_op | source)
XLA Modules:
  0.0 78.4 jit_solution(13063082649345217722)
XLA Ops:
  0.6 76.1 %pair_backward.1.packed = bf16[6,128,128]{2,1,0:T(8,128)(2,1)} custom-call(s32[1,128]{1,0:T(1,128)} %bitcast.2, bf16[128,128]{1,0:T(8,128)(2,1)} %q_h.1, bf16[128,128]{1,0:T(8,128)(2,1)} %k_h.1, bf16[128,128]{1,0:T(8,128)(2,1)} %v_h.1, bf16[128,128]{1,0:T(8,128)(2,1)} %hq_h.1, bf16[128,128]{1,0:T(8,128)(2,1)} %hv_h.1, bf16[128,128]{1,0:T(8,128)(2,1)} %taps_h.1, ...), custom_call_target="tpu_custom_call" | custom-call | tf_op jit(solution)/shard_map/pair_backward/pallas_call | solution.py:486
  76.8 1.6 %unpack.1 = (bf16[128,128]{1,0:T(8,128)(2,1)}, bf16[128,128]{1,0:T(8,128)(2,1)}, bf16[128,128]{1,0:T(8,128)(2,1)}, bf16[128,128]{1,0:T(8,128)(2,1)}, bf16[128,128]{1,0:T(8,128)(2,1)}, /*index=5*/bf16[128,128]{1,0:T(8,128)(2,1)}) custom-call(bf16[6,128,128]{2,1,0:T(8,128)(2,1)} %pair_backward.1.packed), custom_call_target="tpu_custom_call" | custom-call | tf_op jit(solution)/shard_map/unpack/pallas_call | solution.py:507

commit v5 on v4

--- a/solution.py
+++ b/solution.py
@@ -78,26 +78,19 @@
 
 
 def long_products(table, steps, wide):
-    totals = [jnp.zeros((T, wide), F32)] * 2
-    for part in range(4):
+    totals = [None, None]
+    for part in (3, 2, 1, 0):
         top = part * 32
-        rows = T - top
-
-        def step(g, sums):
-            p = part * 8 + g
-            out = []
-            for j in (0, 1):
-                pair = [
-                    steps[j, pl.ds(T + top - 4 * p - 2 * u, rows), :].astype(BF16) for u in (0, 1)
-                ]
-                right = table[j, 0:wide, pl.ds(pl.multiple_of(p * 256, 256), 256)]
-                out.append(sums[j] + nt(jnp.concatenate(pair, axis=1), right))
-            return tuple(out)
-
-        sums = lax.fori_loop(0, 8, step, tuple(t[top:] for t in totals), unroll=2)
-        if top:
-            sums = [jnp.concatenate([totals[j][0:top], sums[j]], axis=0) for j in (0, 1)]
-        totals = list(sums)
+        for j in (0, 1):
+            pairs = [
+                steps[j, T + top - d : 2 * T - d, :].astype(BF16) for d in range(top, top + 32, 2)
+            ]
+            right = table[j, 0:wide, part * 2048 : (part + 1) * 2048]
+            now = nt(jnp.concatenate(pairs, axis=1), right)
+            if totals[j] is not None:
+                below = T - top - 32
+                now = jnp.concatenate([now[0:32], now[32 : 32 + below] + totals[j]], axis=0)
+            totals[j] = now
     return totals
 
 
@@ -105,7 +98,7 @@
     order_h, q_h, k_h, v_h, hq_h, hv_h, taps_h, gain_h, up_h,
     packed,
     order_s, order_v, hq_ref, hv_ref, taps_ref, gain_ref, up_ref,
-    q_all, k_all, v_all, vt, kt, scores,
+    q_all, k_all, v_all, vt, kt,
     tg_s, tg, o_s, o_r, os_s, os_r, bm_s, bm, st_s, st_r, sc_s, sc_all, at_s, at_all, ds_s, ds_r, do_all,
     mx_s, mx, cg_s, cg, dq_s, dq_r, dkv_s, dkv_r,
     up_t, hv_t, hvg_t, gain_t, table, chunks, steps, dq_acc,
@@ -213,7 +206,6 @@
     gain_t[...] = jnp.broadcast_to(gain_ref[...], (T, T)).T
     hvg_t[...] = hv_t[...] * gain_t[...]
     steps[:, 0:T, :] = jnp.zeros((2, T, T), F32)
-    dq_acc[...] = jnp.zeros((T, N * T), F32)
 
     lane = iota((T, T), 1)
     line = iota((T, T), 0)
@@ -259,48 +251,51 @@
         base = within & (HALF - 1)
         spot = jnp.zeros((1, 2 * T), jnp.int32)
         for e in range(4):
-            block = order_s[0, ((pair * 2 + e // 2) * N + c) * 2 + e % 2]
+            block = order_s[0, (pair[e // 2] * N + c) * 2 + e % 2]
             spot = jnp.where((within >> 6) == e, block * HALF, spot)
         return spot + base
 
-    def masked(tile, pair_q, spots):
-        keys = k_all[pl.ds(2 * tile, 2)].reshape(2 * T, T)
+    def two(field, pair, axis=0):
+        return jnp.concatenate([field[pair[0]], field[pair[1]]], axis=axis)
+
+    def masked(keys, tile, pair_q, spots):
         raw = nt(keys, pair_q) * (scale * LOG2E)
         out = []
         for e in range(4):
-            block = order_s[0, y * 16 + tile * 4 + e]
+            block = order_s[0, y * 16 + tile[e // 2] * 2 + e % 2]
             out.append(
                 jnp.where(deep <= spots - block * HALF, raw[e * HALF : (e + 1) * HALF], HIDDEN)
             )
         return jnp.concatenate(out, axis=0)
 
-    def attend(turn, _):
-        pair = lax.rem(turn + lax.div(y, 2), 4)
-        pair_q = q_all[pl.ds(pair * 2, 2)].reshape(2 * T, T)
+    fixed = [(2 * t, 2 * t + 1) for t in range(4)]
+
+    def others_first(own):
+        return [tuple(lax.rem(own + 1 + 2 * t + e, N) for e in (0, 1)) for t in range(4)]
+
+    def attend(turn, pair):
+        pair_q = two(q_all, pair)
         spots = query_places(pair)
-        peak = jnp.full((1, 2 * T), HIDDEN, F32)
-        for tile in range(4):
-            part = masked(tile, pair_q, spots)
-            scores[tile * 256 : (tile + 1) * 256, :] = part
-            peak = jnp.maximum(peak, jnp.max(part, axis=0, keepdims=True))
+        parts = [masked(two(k_all, tile), tile, pair_q, spots) for tile in fixed]
+        peak = jnp.max(jnp.maximum(jnp.maximum(parts[0], parts[1]), jnp.maximum(parts[2], parts[3])), axis=0, keepdims=True)
         total = jnp.zeros((1, 2 * T), F32)
         out = jnp.zeros((T, 2 * T), F32)
         for tile in range(4):
-            weights = jnp.exp2(scores[tile * 256 : (tile + 1) * 256, :] - peak)
+            weights = jnp.exp2(parts[tile] - peak)
             total = total + jnp.sum(weights, axis=0, keepdims=True)
             out = out + nn(vt[:, tile * 256 : (tile + 1) * 256], weights.astype(BF16))
         for e in (0, 1):
-            p = pair * 2 + e
+            p = pair[e]
             lanes = slice(e * T, (e + 1) * T)
-            o_s[p] = out[:, lanes].astype(BF16)
-            os_s[p] = jnp.concatenate([peak[:, lanes], total[:, lanes]], axis=0)
-
-            @pl.when(p != y)
-            def _():
+            stats = jnp.concatenate([peak[:, lanes], total[:, lanes]], axis=0)
+            if turn == 3 and e == 1:
+                o_r[y] = out[:, lanes].astype(BF16)
+                os_r[y] = stats
+            else:
+                o_s[p] = out[:, lanes].astype(BF16)
+                os_s[p] = stats
                 os_post(os_s.at[p], y, (p * N + c, head))
                 o_post(o_s.at[p], y, (p * N + c, head))
-
-        return 0
 
     tg_here()
     both_rows = tg[...].reshape(2 * T, T)
@@ -323,12 +318,11 @@
     v_here()
     for i in range(N):
         vt[:, i * T : (i + 1) * T] = flip(v_all[i]).astype(BF16)
-        kt[:, i * T : (i + 1) * T] = flip(k_all[i]).astype(BF16)
+        kt[i] = flip(k_all[i]).astype(BF16)
     os_post, os_here = channel(os_r)
     o_post, o_here = channel(o_r)
-    lax.fori_loop(0, 4, attend, 0)
-    o_r[y] = o_s[y]
-    os_r[y] = os_s[y]
+    for turn, pair in enumerate(others_first(y)):
+        attend(turn, pair)
 
     flats = [jnp.zeros((HALF, T), F32)] * 2
     for h in (0, 1):
@@ -398,41 +392,37 @@
         ).astype(BF16)
     dkv_post, dkv_here = channel(dkv_r)
 
-    def grad(turn, _):
-        tile = lax.rem(turn + lax.div(c, 2), 4)
-        rows = pl.ds(pl.multiple_of(tile * 2 * T, 2 * T), 2 * T)
-        tile_v = v_all[pl.ds(2 * tile, 2)].reshape(2 * T, T)
+    def grad(turn, tile):
+        tile_k, tile_v, tile_kt = two(k_all, tile), two(v_all, tile), two(kt, tile, 1)
         dk = jnp.zeros((2 * T, T), F32)
         dv = jnp.zeros((2 * T, T), F32)
-        for pair in range(4):
-            pair_q = q_all[pair * 2 : pair * 2 + 2].reshape(2 * T, T)
-            pair_do = jnp.concatenate([do_all[pair * 2], do_all[pair * 2 + 1]], axis=1)
-            both = jnp.concatenate([ds_r[pair * 2], ds_r[pair * 2 + 1]], axis=1)
-            probs = jnp.exp2(masked(tile, pair_q, query_places(pair)) - both[0:1, :])
+        for pair in fixed:
+            pair_q = two(q_all, pair)
+            pair_do = two(do_all, pair, 1)
+            both = two(ds_r, pair, 1)
+            lanes = slice(pair[0] * T, (pair[1] + 1) * T)
+            probs = jnp.exp2(masked(tile_k, tile, pair_q, query_places(pair)) - both[0:1, :])
             dprobs = nn(tile_v, pair_do)
             dscores = (probs * (dprobs - both[1:2, :])).astype(BF16)
             dv = dv + nt(probs.astype(BF16), pair_do)
             dk = dk + nn(dscores, pair_q)
-            dq_acc[:, pair * 2 * T : (pair + 1) * 2 * T] += nn(kt[:, rows], dscores)
-        dk = (dk * scale).astype(BF16)
-        dv = dv.astype(BF16)
+            part = nn(tile_kt, dscores)
+            dq_acc[:, lanes] = part if turn == 0 else dq_acc[:, lanes] + part
+        dkv = (dk * scale).astype(BF16), dv.astype(BF16)
         for e in (0, 1):
-            p = tile * 2 + e
-            dkv_s[p, 0:T, :] = dk[e * T : (e + 1) * T]
-            dkv_s[p, T : 2 * T, :] = dv[e * T : (e + 1) * T]
-
-            @pl.when(p != c)
-            def _():
+            p = tile[e]
+            own = turn == 3 and e == 1
+            for i, field in enumerate(dkv):
+                (dkv_r if own else dkv_s)[p, i * T : (i + 1) * T, :] = field[e * T : (e + 1) * T]
+            if not own:
                 dkv_post(dkv_s.at[p], c, (y * N + p, head))
 
-        return 0
-
-    lax.fori_loop(0, 4, grad, 0)
+    for turn, tile in enumerate(others_first(c)):
+        grad(turn, tile)
     for i in range(N):
         dq_s[i] = (dq_acc[:, i * T : (i + 1) * T] * scale).astype(BF16)
     dq_here = spread(y_peer, lambda p: dq_s.at[p], dq_r, y)
     dq_r[y] = dq_s[y]
-    dkv_r[c] = dkv_s[c]
 
     mx_here()
     lay_out(mx[...].reshape(T, T), True, False)
@@ -490,7 +480,7 @@
         out_specs=pl.BlockSpec(memory_space=pltpu.VMEM),
         scratch_shapes=[
             pltpu.SMEM((1, T), jnp.int32), vmem(1, T, dtype=jnp.int32), one, one, one, vmem(1, T, dtype=F32), one,
-            square, square, square, vmem(T, N * T), vmem(T, N * T), vmem(N * T, 2 * T, dtype=F32),
+            square, square, square, vmem(T, N * T), square,
             fours, fours, square, square, lines, lines, twos, twos, vmem(2, T, dtype=F32), lines,
             one, square, one, square, vmem(4, T, dtype=F32), vmem(N, 4, T, dtype=F32), square,
             twos, twos, fours, fours, square, square, tall, tall,

time: 78.6 us -> 76.8 us (0.977)
  Pallas kernels: 77.7 us -> 75.8 us
    pallas_call x1, Pallas kernels: 76.1 us -> 74.2 us  [per_device(): pl.pallas_call(kernel, out_shape=jax.ShapeDtypeStruct((6, T, T), BF16), i...]
where the time goes in v5:
time: 76.8 us; the launch traced here: 76.5 us
  Pallas kernels  75.8 us (99%)
    pallas_call x1, Pallas kernels, per_device(): pl.pallas_call(kernel, out_shape=jax.ShapeDtypeStruct((6, T, T), BF16), i...  74.2 us
    pallas_call x1, Pallas kernels, per_device(): pl.pallas_call(unpack, out_shape=(jax.ShapeDtypeStruct((T, T), BF16),) *...  1.6 us

profile of v5, /device:TPU:1, one launch (start us, length us, event | category | flops | bytes accessed | tf_op | source)
XLA Modules:
  0.0 76.5 jit_solution(13688165612696469287)
XLA Ops:
  0.6 74.2 %pair_backward.1.packed = bf16[6,128,128]{2,1,0:T(8,128)(2,1)} custom-call(s32[1,128]{1,0:T(1,128)} %bitcast.2, bf16[128,128]{1,0:T(8,128)(2,1)} %q_h.1, bf16[128,128]{1,0:T(8,128)(2,1)} %k_h.1, bf16[128,128]{1,0:T(8,128)(2,1)} %v_h.1, bf16[128,128]{1,0:T(8,128)(2,1)} %hq_h.1, bf16[128,128]{1,0:T(8,128)(2,1)} %hv_h.1, bf16[128,128]{1,0:T(8,128)(2,1)} %taps_h.1, ...), custom_call_target="tpu_custom_call" | custom-call | tf_op jit(solution)/shard_map/pair_backward/pallas_call | solution.py:476
  74.9 1.6 %unpack.1 = (bf16[128,128]{1,0:T(8,128)(2,1)}, bf16[128,128]{1,0:T(8,128)(2,1)}, bf16[128,128]{1,0:T(8,128)(2,1)}, bf16[128,128]{1,0:T(8,128)(2,1)}, bf16[128,128]{1,0:T(8,128)(2,1)}, /*index=5*/bf16[128,128]{1,0:T(8,128)(2,1)}) custom-call(bf16[6,128,128]{2,1,0:T(8,128)(2,1)} %pair_backward.1.packed), custom_call_target="tpu_custom_call" | custom-call | tf_op jit(solution)/shard_map/unpack/pallas_call | solution.py:497

commit v6 on v5

--- a/solution.py
+++ b/solution.py
@@ -74,7 +74,7 @@
         return tuple(after)
 
     empty = jnp.zeros((HALF, T), F32)
-    lax.fori_loop(0, SEQ // T, step, (empty, empty), unroll=4)
+    lax.fori_loop(0, SEQ // T, step, (empty, empty), unroll=16)
 
 
 def long_products(table, steps, wide):
@@ -102,7 +102,7 @@
     tg_s, tg, o_s, o_r, os_s, os_r, bm_s, bm, st_s, st_r, sc_s, sc_all, at_s, at_all, ds_s, ds_r, do_all,
     mx_s, mx, cg_s, cg, dq_s, dq_r, dkv_s, dkv_r,
     up_t, hv_t, hvg_t, gain_t, table, chunks, steps, dq_acc,
-    send, recv, load, grid_sem,
+    outs, send, recv, load, grid_sem, store,
 ):
     me = lax.axis_index("ctx")
     head = lax.axis_index("ch")
@@ -173,6 +173,7 @@
     for peer in (c_peer, y_peer, h_peer):
         lax.fori_loop(1, N, greet(barrier, peer), 0)
 
+    moves = [pltpu.make_async_copy(outs.at[i], packed.at[i], store.at[i]) for i in range(6)]
     loads = [
         pltpu.make_async_copy(src, dst, load.at[i])
         for i, (src, dst) in enumerate(
@@ -324,6 +325,13 @@
     for turn, pair in enumerate(others_first(y)):
         attend(turn, pair)
 
+    bm_here()
+    back = bm[...].reshape(T, T).astype(F32)
+    sc_s[...] = (back * hvg_t[...]).astype(BF16)
+    sc_all[y] = sc_s[...]
+    sc_here = spread(y_peer, lambda p: sc_s, sc_all, y)
+    scaled = sc_s[...].astype(F32)
+
     flats = [jnp.zeros((HALF, T), F32)] * 2
     for h in (0, 1):
         for hh in (0, 1):
@@ -335,13 +343,6 @@
     for j in (0, 1):
         chunks[j] = flats[j]
     toeplitz(chunks, table, HALF)
-
-    bm_here()
-    back = bm[...].reshape(T, T).astype(F32)
-    sc_s[...] = (back * hvg_t[...]).astype(BF16)
-    sc_all[y] = sc_s[...]
-    sc_here = spread(y_peer, lambda p: sc_s, sc_all, y)
-    scaled = sc_s[...].astype(F32)
 
     os_here()
     o_here()
@@ -381,7 +382,8 @@
     mx_s[...] = (normed * hv_t[...]).astype(BF16).reshape(N * N, 2, T)
     mx[me] = mx_s[me]
     mx_here = spread(all_peer, lambda p: mx_s.at[p], mx, me)
-    packed[4] = flip((back * normed).astype(BF16)).astype(BF16)
+    outs[4] = flip((back * normed).astype(BF16)).astype(BF16)
+    moves[4].start()
 
     sc_here()
     at_here()
@@ -438,22 +440,29 @@
     grad_q = dq_r[0].astype(F32)
     for i in range(1, N):
         grad_q = grad_q + dq_r[i].astype(F32)
-    packed[0] = grad_q.T.astype(BF16)
+    outs[0] = grad_q.T.astype(BF16)
+    moves[0].start()
     dkv_here()
     grad_kv = dkv_r[0].astype(F32)
     for i in range(1, N):
         grad_kv = grad_kv + dkv_r[i].astype(F32)
-    packed[1] = grad_kv[0:T].astype(BF16)
-    packed[2] = grad_kv[T : 2 * T].astype(BF16)
+    outs[1] = grad_kv[0:T].astype(BF16)
+    moves[1].start()
+    outs[2] = grad_kv[T : 2 * T].astype(BF16)
+    moves[2].start()
 
     cg_here()
     results = cg[...].reshape(2 * T, T)
-    packed[3] = flip(up_t[...] * separate(results, 0).astype(F32)).astype(BF16)
-    packed[5] = flip(separate(results, 1)).astype(BF16)
+    outs[3] = flip(up_t[...] * separate(results, 0).astype(F32)).astype(BF16)
+    moves[3].start()
+    outs[5] = flip(separate(results, 1)).astype(BF16)
+    moves[5].start()
 
     for sem, dst in enumerate(started):
         part = dst.at[pl.ds(0, dst.shape[0] - 1)]
         pltpu.make_async_copy(part, part, send.at[sem]).wait()
+    for move in moves:
+        move.wait()
 
 
 def unpack(packed, *outs):
@@ -477,7 +486,7 @@
         kernel,
         out_shape=jax.ShapeDtypeStruct((6, T, T), BF16),
         in_specs=[in_hbm] * 9,
-        out_specs=pl.BlockSpec(memory_space=pltpu.VMEM),
+        out_specs=in_hbm,
         scratch_shapes=[
             pltpu.SMEM((1, T), jnp.int32), vmem(1, T, dtype=jnp.int32), one, one, one, vmem(1, T, dtype=F32), one,
             square, square, square, vmem(T, N * T), square,
@@ -486,8 +495,8 @@
             twos, twos, fours, fours, square, square, tall, tall,
             wide, wide, wide, wide, vmem(2, T, SEQ), vmem(2, HALF, T, dtype=F32), vmem(2, 2 * T, T, dtype=F32),
             vmem(T, N * T, dtype=F32),
-            pltpu.SemaphoreType.DMA((15,)), pltpu.SemaphoreType.DMA((15,)), pltpu.SemaphoreType.DMA((10,)),
-            pltpu.SemaphoreType.REGULAR,
+            vmem(6, T, T), pltpu.SemaphoreType.DMA((15,)), pltpu.SemaphoreType.DMA((15,)), pltpu.SemaphoreType.DMA((10,)),
+            pltpu.SemaphoreType.REGULAR, pltpu.SemaphoreType.DMA((6,)),
         ],
         compiler_params=pltpu.CompilerParams(
             collective_id=0, has_side_effects=True, vmem_limit_bytes=60 * 1024 * 1024

time: 76.8 us -> 77.2 us (level)
  no operation moved by 1% of the time
where the time goes in v6:
time: 77.2 us; the launch traced here: 76.9 us
  Pallas kernels  76.3 us (99%)
    pallas_call x1, Pallas kernels, per_device(): pl.pallas_call(kernel, out_shape=jax.ShapeDtypeStruct((6, T, T), BF16), i...  74.7 us
    pallas_call x1, Pallas kernels, per_device(): pl.pallas_call(unpack, out_shape=(jax.ShapeDtypeStruct((T, T), BF16),) *...  1.6 us

profile of v6, /device:TPU:1, one launch (start us, length us, event | category | flops | bytes accessed | tf_op | source)
XLA Modules:
  0.0 76.9 jit_solution(14312116899329676216)
XLA Ops:
  0.6 74.7 %pair_backward.1.packed = bf16[6,128,128]{2,1,0:T(8,128)(2,1)} custom-call(s32[1,128]{1,0:T(1,128)} %bitcast.2, bf16[128,128]{1,0:T(8,128)(2,1)} %q_h.1, bf16[128,128]{1,0:T(8,128)(2,1)} %k_h.1, bf16[128,128]{1,0:T(8,128)(2,1)} %v_h.1, bf16[128,128]{1,0:T(8,128)(2,1)} %hq_h.1, bf16[128,128]{1,0:T(8,128)(2,1)} %hv_h.1, bf16[128,128]{1,0:T(8,128)(2,1)} %taps_h.1, ...), custom_call_target="tpu_custom_call" | custom-call | tf_op jit(solution)/shard_map/pair_backward/pallas_call | solution.py:485
  75.3 1.6 %unpack.1 = (bf16[128,128]{1,0:T(8,128)(2,1)}, bf16[128,128]{1,0:T(8,128)(2,1)}, bf16[128,128]{1,0:T(8,128)(2,1)}, bf16[128,128]{1,0:T(8,128)(2,1)}, bf16[128,128]{1,0:T(8,128)(2,1)}, /*index=5*/bf16[128,128]{1,0:T(8,128)(2,1)}) custom-call(bf16[6,128,128]{2,1,0:T(8,128)(2,1)} %pair_backward.1.packed), custom_call_target="tpu_custom_call" | custom-call | tf_op jit(solution)/shard_map/unpack/pallas_call | solution.py:506
